TPU v7x, 32 devices: a whole 2x2x4 slice. The times are simulated.
32 devices in a mesh: fsdp: 8 (over z, x), ctx: 4 (over y, core).
Axes of the slice: x: 2, y: 2, z: 4, core: 2. Of those that a mesh axis runs over, the one named last changes fastest.
Arguments:
- hidden_in: bfloat16 [8, 1536, 768], P('fsdp', 'ctx'), may hold values from -6 to 6
- segment_ids: int32 [8, 1536], P('fsdp', 'ctx'), may hold values from 0 to 2, as said below
- positions: int32 [8, 1536], P('fsdp', 'ctx'), may hold values from 0 to 2556, as said below
- norm1_gain: bfloat16 [768], P('fsdp'), may hold values from 0.5 to 1.5
- qkv_weight: bfloat16 [768, 2304], P('fsdp'), may hold values from -0.21875 to 0.21875
- out_weight: bfloat16 [768, 768], P('fsdp'), may hold values from -6 to 6
- norm2_gain: bfloat16 [768], P('fsdp'), may hold values from 0.5 to 1.5
- in_weight: bfloat16 [768, 2304], P('fsdp'), may hold values from -0.21875 to 0.21875
- down_weight: bfloat16 [1152, 768], P('fsdp'), may hold values from -0.375 to 0.375
- out_cot: bfloat16 [8, 1536, 768], P('fsdp', 'ctx'), may hold values from -6 to 6
Outputs:
- out: bfloat16 [8, 1536, 768], P('fsdp', 'ctx')
- in_grad: float32 [8, 1536, 768], P('fsdp', 'ctx')
- norm1_gain_grad: float32 [768], P('fsdp')
- qkv_weight_grad: float32 [768, 2304], P('fsdp')
- out_weight_grad: float32 [768, 768], P('fsdp')
- norm2_gain_grad: float32 [768], P('fsdp')
- in_weight_grad: float32 [768, 2304], P('fsdp')
- down_weight_grad: float32 [1152, 768], P('fsdp')
Inputs may be any that keep to these rules, and one draw needn't show every extreme that they name: `segment_ids`: in each sequence the ids never fall: 0 on its first tokens, 1 from a place within the first 384 tokens to a place within the last 384, 2 on the tokens after it. Within a document the positions rise by one from token to token; the first document of each sequence starts at 0, the second ends at 2556, the third starts at some value below 1024.
All inputs are finite; a program needn't handle non-finite values.
Results may differ from a plain program's by a relative error of at most 0.015.
Values may be sent and summed in bfloat16 or wider, within the bound.
No kernel may reach another device: no remote copies, remote signals or barrier semaphores. Data moves between devices by JAX's collectives and lax.ppermute only.
A program may use at most 256 MiB of HBM per device.

v0:
```python
import jax
import jax.numpy as jnp
from jax import lax
from jax.sharding import PartitionSpec as P

HEADS = 12
HEAD_DIM = 64


rope_base = 160000.0
norm_eps = 1e-05
masked_score = -1e30


def from_behind(shard, axis, by):
    count = lax.axis_size(axis)
    return lax.ppermute(shard, axis, [(i, (i + by) % count) for i in range(count)])


def normalize(fields):
    row_mean = jnp.mean(fields, axis=-1, keepdims=True)
    centred = fields - row_mean
    variance = jnp.mean(centred * centred, axis=-1, keepdims=True)
    inv_root = lax.rsqrt(variance + norm_eps)
    return (centred * inv_root, inv_root)


def norm_back(grad_out, normed, inv_root, gain):
    scaled = grad_out * gain.astype(jnp.float32)
    return inv_root * (
        scaled
        - jnp.mean(scaled, axis=-1, keepdims=True)
        - normed * jnp.mean(scaled * normed, axis=-1, keepdims=True)
    )


def rope_tables(places):
    half_dim = HEAD_DIM // 2
    frequency = rope_base ** (-2.0 * jnp.arange(half_dim, dtype=jnp.float32) / HEAD_DIM)
    angles = places.astype(jnp.float32)[:, None] * frequency[None, :]
    return (jnp.cos(angles)[:, None, :], jnp.sin(angles)[:, None, :])


def rotate(fields, cosine_table, sine_table):
    half_dim = HEAD_DIM // 2
    lower_half = fields[..., :half_dim]
    upper_half = fields[..., half_dim:]
    return jnp.concatenate(
        [
            lower_half * cosine_table - upper_half * sine_table,
            upper_half * cosine_table + lower_half * sine_table,
        ],
        axis=-1,
    )


def split_heads(flat):
    return flat.reshape(flat.shape[0], HEADS, HEAD_DIM)


def exact_gelu(values):
    return jax.nn.gelu(values, approximate=False)


def block_scores(rows_low, cols_low, row_docs, col_docs):
    scores = jnp.einsum(
        "qhe,khe->hqk",
        split_heads(rows_low),
        split_heads(cols_low),
        preferred_element_type=jnp.float32,
    ) * HEAD_DIM ** (-0.5)
    return jnp.where((row_docs[:, None] == col_docs[None, :])[None], scores, masked_score)


def pair_terms(
    query_rows, acc_rows, key_piece, value_piece, row_docs, col_docs, maxima, scaled_delta
):
    scores = block_scores(query_rows, key_piece, row_docs, col_docs)
    expo_f = jnp.exp(scores - maxima[:, :, None])
    grad_prob = jnp.einsum(
        "qhe,khe->hqk", acc_rows, split_heads(value_piece), preferred_element_type=jnp.float32
    )
    grad_score = (expo_f * (grad_prob - scaled_delta[:, :, None])).astype(jnp.bfloat16)
    return (expo_f.astype(jnp.bfloat16), grad_score)


def body(
    hidden_in,
    segment_ids,
    positions,
    norm1_gain,
    qkv_weight,
    out_weight,
    norm2_gain,
    in_weight,
    down_weight,
    out_cot,
):
    model_width = hidden_in.shape[-1]
    inputs = hidden_in.reshape(-1, model_width)
    local_rows = inputs.shape[0]
    own_docs = segment_ids.reshape(-1)
    gain_one, w_qkv, w_out = (
        lax.all_gather(norm1_gain, "fsdp", axis=0, tiled=True),
        lax.all_gather(qkv_weight, "fsdp", axis=0, tiled=True),
        lax.all_gather(out_weight, "fsdp", axis=0, tiled=True),
    )
    gain_two, w_in, w_down = (
        lax.all_gather(norm2_gain, "fsdp", axis=0, tiled=True),
        lax.all_gather(in_weight, "fsdp", axis=0, tiled=True),
        lax.all_gather(down_weight, "fsdp", axis=0, tiled=True),
    )
    all_docs = lax.all_gather(own_docs, "ctx", axis=0, tiled=True)
    ff_width = w_down.shape[0]
    cosine_table, sine_table = rope_tables(positions.reshape(-1))
    resid_in = inputs.astype(jnp.float32)
    normed_one, inv_one = normalize(resid_in)
    h_one = (normed_one * gain_one.astype(jnp.float32)).astype(jnp.bfloat16)
    qkv_proj = jnp.dot(h_one, w_qkv, preferred_element_type=jnp.float32)
    query_low = (
        rotate(split_heads(qkv_proj[:, :model_width]), cosine_table, sine_table)
        .astype(jnp.bfloat16)
        .reshape(local_rows, model_width)
    )
    key_low = (
        rotate(split_heads(qkv_proj[:, model_width : 2 * model_width]), cosine_table, sine_table)
        .astype(jnp.bfloat16)
        .reshape(local_rows, model_width)
    )
    value_low = qkv_proj[:, 2 * model_width :].astype(jnp.bfloat16)
    own_max = jnp.max(block_scores(query_low, key_low, own_docs, own_docs), axis=-1)
    key_piece = lax.all_gather(key_low, "ctx", axis=0, tiled=True)
    value_piece = lax.all_gather(value_low, "ctx", axis=0, tiled=True)
    col_docs = all_docs
    scores = block_scores(query_low, key_piece, own_docs, col_docs)
    expo_f = jnp.exp(scores - own_max[:, :, None])
    total = jnp.sum(expo_f, axis=-1)
    acc = jnp.einsum(
        "hqk,khe->qhe",
        expo_f.astype(jnp.bfloat16),
        split_heads(value_piece),
        preferred_element_type=jnp.float32,
    )
    acc, total = (acc, total)
    mixed_f = acc / total.T[:, :, None]
    mixed_low = mixed_f.reshape(local_rows, model_width).astype(jnp.bfloat16)
    resid = resid_in + jnp.dot(mixed_low, w_out, preferred_element_type=jnp.float32)
    normed_two, inv_two = normalize(resid)
    h_two = (normed_two * gain_two.astype(jnp.float32)).astype(jnp.bfloat16)
    up_all = jnp.dot(h_two, w_in, preferred_element_type=jnp.float32)
    gate_part = up_all[:, :ff_width]
    up_part = up_all[:, ff_width:]
    gelu_gate, gelu_pullback = jax.vjp(exact_gelu, gate_part)
    mid_low = (gelu_gate * up_part).astype(jnp.bfloat16)
    output = resid + jnp.dot(mid_low, w_down, preferred_element_type=jnp.float32)
    out = output.astype(jnp.bfloat16).reshape(hidden_in.shape)
    cotangent = out_cot.reshape(local_rows, model_width).astype(jnp.float32)
    grad_branch = cotangent.astype(jnp.bfloat16)
    grad_down = jnp.einsum("tf,td->fd", mid_low, grad_branch, preferred_element_type=jnp.float32)
    grad_mid = jnp.einsum("td,fd->tf", grad_branch, w_down, preferred_element_type=jnp.float32)
    grad_gate = gelu_pullback(grad_mid * up_part)[0]
    grad_u = jnp.concatenate([grad_gate, grad_mid * gelu_gate], axis=1).astype(jnp.bfloat16)
    grad_in = jnp.einsum("td,tf->df", h_two, grad_u, preferred_element_type=jnp.float32)
    grad_h_two = jnp.einsum("tf,df->td", grad_u, w_in, preferred_element_type=jnp.float32)
    grad_gain_two = jnp.sum(grad_h_two * normed_two, axis=0)
    grad_resid = cotangent + norm_back(grad_h_two, normed_two, inv_two, gain_two)
    grad_attn = grad_resid.astype(jnp.bfloat16)
    grad_out = jnp.einsum("td,te->de", mixed_low, grad_attn, preferred_element_type=jnp.float32)
    grad_mixed = split_heads(
        jnp.einsum("te,de->td", grad_attn, w_out, preferred_element_type=jnp.float32)
    )
    grad_acc = (grad_mixed / total.T[:, :, None]).astype(jnp.bfloat16)
    row_delta = jnp.sum(grad_mixed * mixed_f, axis=-1).T
    scaled_delta = row_delta / total
    query_heads = split_heads(query_low)
    zero_heads = jnp.zeros((local_rows, HEADS, HEAD_DIM), jnp.float32)
    cycle_size = lax.axis_size("ctx")
    my_index = lax.axis_index("ctx")

    def cycle_turn(turn, carried):
        grad_query, blocks, grads = carried
        key_piece = blocks[0]
        value_piece = blocks[1]
        source = jnp.mod(my_index - turn, cycle_size)
        col_docs = lax.dynamic_slice_in_dim(all_docs, source * local_rows, local_rows)
        expo_low, grad_score = pair_terms(
            query_low, grad_acc, key_piece, value_piece, own_docs, col_docs, own_max, scaled_delta
        )
        grad_query = grad_query + jnp.einsum(
            "hqk,khe->qhe", grad_score, split_heads(key_piece), preferred_element_type=jnp.float32
        )
        grad_key_part = jnp.einsum(
            "hqk,qhe->khe", grad_score, query_heads, preferred_element_type=jnp.float32
        )
        grad_value_part = jnp.einsum(
            "hqk,qhe->khe", expo_low, grad_acc, preferred_element_type=jnp.float32
        )
        grads = grads + jnp.stack([grad_key_part, grad_value_part])
        blocks = from_behind(blocks, "ctx", 1)
        grads = from_behind(grads, "ctx", 1)
        return (grad_query, blocks, grads)

    start_cycle = (zero_heads, jnp.stack([key_low, value_low]), jnp.stack([zero_heads, zero_heads]))
    grad_query, returned_blocks, grads = lax.fori_loop(0, cycle_size, cycle_turn, start_cycle)
    grad_key = grads[0]
    grad_value = grads[1]
    score_scale = HEAD_DIM ** (-0.5)
    grad_qkv = jnp.concatenate(
        [
            rotate(grad_query * score_scale, cosine_table, -sine_table).reshape(
                local_rows, model_width
            ),
            rotate(grad_key * score_scale, cosine_table, -sine_table).reshape(
                local_rows, model_width
            ),
            grad_value.reshape(local_rows, model_width),
        ],
        axis=1,
    ).astype(jnp.bfloat16)
    grad_qkv_w = jnp.einsum("td,tf->df", h_one, grad_qkv, preferred_element_type=jnp.float32)
    grad_h_one = jnp.einsum("tf,df->td", grad_qkv, w_qkv, preferred_element_type=jnp.float32)
    grad_gain_one = jnp.sum(grad_h_one * normed_one, axis=0)
    grad_input = grad_resid + norm_back(grad_h_one, normed_one, inv_one, gain_one)
    in_grad = grad_input.reshape(hidden_in.shape)
    grad_list = (grad_gain_one, grad_qkv_w, grad_out, grad_gain_two, grad_in, grad_down)
    shares = (
        lax.psum_scatter(grad_list[0], "fsdp", scatter_dimension=0, tiled=True),
        lax.psum_scatter(grad_list[1], "fsdp", scatter_dimension=0, tiled=True),
        lax.psum_scatter(grad_list[2], "fsdp", scatter_dimension=0, tiled=True),
        lax.psum_scatter(grad_list[3], "fsdp", scatter_dimension=0, tiled=True),
        lax.psum_scatter(grad_list[4], "fsdp", scatter_dimension=0, tiled=True),
        lax.psum_scatter(grad_list[5], "fsdp", scatter_dimension=0, tiled=True),
    )
    totals = lax.psum((shares[0], shares[1], shares[2], shares[3], shares[4], shares[5]), "ctx")
    return (out, in_grad, totals[0], totals[1], totals[2], totals[3], totals[4], totals[5])


def solution(mesh):
    placed = (
        P("fsdp", "ctx", None),
        P("fsdp", "ctx"),
        P("fsdp", "ctx"),
        P("fsdp"),
        P("fsdp", None),
        P("fsdp", None),
        P("fsdp"),
        P("fsdp", None),
        P("fsdp", None),
        P("fsdp", "ctx", None),
    )
    return jax.shard_map(
        body,
        mesh=mesh,
        in_specs=placed,
        out_specs=(
            P("fsdp", "ctx", None),
            P("fsdp", "ctx", None),
            P("fsdp"),
            P("fsdp", None),
            P("fsdp", None),
            P("fsdp"),
            P("fsdp", None),
            P("fsdp", None),
        ),
        check_vma=False,
    )
```

profile of v0, /device:TPU:0, one launch (start us, length us, event | category | flops | bytes accessed | tf_op | source)
XLA Modules:
  0.0 792.3 jit_solution(2541296478649146400)
XLA Ops:
  11.6 23.2 %all-reduce.7 = (bf16[768]{0:T(1024)(128)(2,1)S(1)}, bf16[768]{0:T(1024)(128)(2,1)S(1)}) all-reduce(bf16[768]{0:T(1024)(128)(2,1)S(1)} %dynamic-update-slice, bf16[768]{0:T(1024)(128)(2,1)S(1)} %dynamic-update-slice.1), channel_id=1, replica_groups=mesh['fsdp'=8,'ctx'=4] {'fsdp'}, use_global_device_ids=true, to_apply=%add | all-reduce | flops 1536 | bytes 6144
  39.1 39.2 %all-gather.8.cloned.1.call-done = bf16[768,2304]{1,0:T(8,128)(2,1)} async-done(((bf16[96,2304]{1,0:T(8,128)(2,1)}), bf16[768,2304]{1,0:T(8,128)(2,1)}) %all-gather.8.cloned.1.call-update) | async-done | bytes 3538960 | tf_op jit(solution)/shard_map/all_gather | solution.py:105
  78.3 3.6 fusion.66
  89.5 5.2 all-gather
  99.8 8.4 %all-gather.12.cloned.1.call-done = bf16[1536,768]{0,1:T(8,128)(2,1)} async-done(((bf16[384,768]{0,1:T(8,128)(2,1)}), bf16[1536,768]{0,1:T(8,128)(2,1)}) %all-gather.12.cloned.1.call-update) | async-done | bytes 2359312 | tf_op jit(solution)/shard_map/all_gather | solution.py:132
  108.2 15.3 %fusion.10 = (f32[12,384]{1,0:T(8,128)S(1)}, f32[12,384,1536]{2,1,0:T(8,128)}) fusion(f32[12,384]{1,0:T(8,128)} %select_reduce_fusion, pred[384,1536]{1,0:T(8,128)(4,1)S(1)} %copy-done.30, bf16[1536,12,64]{0,2,1:T(8,128)(2,1)} %bitcast.157, bf16[384,12,32]{0,2,1:T(8,128)(2,1)S(1)} %get-tuple-element.396, bf16[384,12,32]{0,2,1:T(8,128)(2,1)S(1)} %get-tuple-element.395), kind=kOutput, calls=%fused_computation.14 | convolution fusion | flops 935456256 | bytes 31887360 | tf_op jit(solution)/shard_map/qhe,khe->hqk/dot_general | solution.py:66
  123.5 10.9 %all-gather.10.cloned.1.call-done = bf16[1536,768]{1,0:T(8,128)(2,1)} async-done(((bf16[384,768]{1,0:T(8,128)(2,1)}), bf16[1536,768]{1,0:T(8,128)(2,1)}) %all-gather.10.cloned.1.call-update) | async-done | bytes 2359312 | tf_op jit(solution)/shard_map/all_gather | solution.py:133
  134.4 4.3 copy.32
  138.8 14.1 %fusion.74 = (bf16[384,12,64]{0,2,1:T(8,128)(2,1)S(1)}, f32[384,12,64]{0,2,1:T(8,128)}) fusion(f32[384,12]{0,1:T(8,128)S(1)} %bitcast.155, bf16[1536,12,64]{0,2,1:T(8,128)(2,1)} %bitcast.152, f32[12,384,1536]{2,1,0:T(8,128)} %get-tuple-element.409, f32[12,384]{1,0:T(8,128)} %select_reduce_fusion, pred[384,1536]{1,0:T(8,128)(4,1)S(1)} %copy-done.30), kind=kOutput, calls=%fused_computation.131 | convolution fusion | flops 934871040 | bytes 33067008 | tf_op jit(solution)/shard_map/hqk,khe->qhe/dot_general | solution.py:138
  152.8 24.8 %all-gather.14.cloned.1.call-done = bf16[768,768]{1,0:T(8,128)(2,1)} async-done(((bf16[96,768]{1,0:T(8,128)(2,1)}), bf16[768,768]{1,0:T(8,128)(2,1)}) %all-gather.14.cloned.1.call-update) | async-done | bytes 1179664 | tf_op jit(solution)/shard_map/all_gather | solution.py:106
  180.0 63.7 %all-gather.16.cloned.1.call-done = bf16[768,2304]{1,0:T(8,128)(2,1)} async-done(((bf16[96,2304]{1,0:T(8,128)(2,1)}), bf16[768,2304]{1,0:T(8,128)(2,1)}) %all-gather.16.cloned.1.call-update) | async-done | bytes 3538960 | tf_op jit(solution)/shard_map/all_gather | solution.py:110
  243.7 5.4 fusion.69
  249.0 41.1 %all-gather.18.cloned.1.call-done = bf16[1152,768]{1,0:T(8,128)(2,1)} async-done(((bf16[144,768]{1,0:T(8,128)(2,1)}), bf16[1152,768]{1,0:T(8,128)(2,1)}) %all-gather.18.cloned.1.call-update) | async-done | bytes 1769488 | tf_op jit(solution)/shard_map/all_gather | solution.py:111
  290.2 7.2 add_convert_fusion
  306.0 3.9 fusion.50
  313.9 2.5 copy.37
  321.2 5.1 fusion.43
  328.0 243.3 %while.20 = (s32[]{:T(128)}, f32[384,12,64]{0,2,1:T(8,128)}, bf16[2,384,768]{1,2,0:T(8,128)(2,1)}, f32[2,384,12,64]{1,3,2,0:T(8,128)}, s32[1,384]{1,0:T(1,128)S(...) while((s32[]{:T(128)}, f32[384,12,64]{0,2,1:T(8,128)}, ...), condition=%wide.region_10.11_spmd.clone, body=%wide.region_9.10_spmd.clone.sunk | while | flops 1152073728 | bytes 71949816 | solution.py:204
  335.3 3.2 fusion.128
  338.5 3.9 multiply_convert_fusion.7
  344.2 3.5 maximum_add_fusion.2
  349.1 3.5 fusion.127
  352.6 36.3 %collective-permute-done = bf16[2,384,768]{1,2,0:T(8,128)(2,1)} collective-permute-done((bf16[2,384,768]{1,2,0:T(8,128)(2,1)}, bf16[2,384,768]{1,2,0:T(8,128)(2,1)}, u32[]{:S(2)}, u32[]{:S(2)}) %collective-permute-start) | collective-permute-done | bytes 1179680 | tf_op jit(solution)/shard_map/while/body/eval_jaxpr/ppermute | solution.py:17
  396.0 3.2 fusion.128
  399.2 3.9 multiply_convert_fusion.7
  404.8 3.5 maximum_add_fusion.2
  409.7 3.9 fusion.127
  413.7 35.8 %collective-permute-done = bf16[2,384,768]{1,2,0:T(8,128)(2,1)} collective-permute-done((bf16[2,384,768]{1,2,0:T(8,128)(2,1)}, bf16[2,384,768]{1,2,0:T(8,128)(2,1)}, u32[]{:S(2)}, u32[]{:S(2)}) %collective-permute-start) | collective-permute-done | bytes 1179680 | tf_op jit(solution)/shard_map/while/body/eval_jaxpr/ppermute | solution.py:17
  449.5 2.4 copy.47
  456.6 3.2 fusion.128
  459.8 3.9 multiply_convert_fusion.7
  465.4 3.9 maximum_add_fusion.2
  470.8 3.9 fusion.127
  474.7 35.9 %collective-permute-done = bf16[2,384,768]{1,2,0:T(8,128)(2,1)} collective-permute-done((bf16[2,384,768]{1,2,0:T(8,128)(2,1)}, bf16[2,384,768]{1,2,0:T(8,128)(2,1)}, u32[]{:S(2)}, u32[]{:S(2)}) %collective-permute-start) | collective-permute-done | bytes 1179680 | tf_op jit(solution)/shard_map/while/body/eval_jaxpr/ppermute | solution.py:17
  510.6 2.4 copy.47
  517.7 3.2 fusion.128
  520.9 3.9 multiply_convert_fusion.7
  526.5 3.6 maximum_add_fusion.2
  531.6 3.9 fusion.127
  535.5 35.8 %collective-permute-done = bf16[2,384,768]{1,2,0:T(8,128)(2,1)} collective-permute-done((bf16[2,384,768]{1,2,0:T(8,128)(2,1)}, bf16[2,384,768]{1,2,0:T(8,128)(2,1)}, u32[]{:S(2)}, u32[]{:S(2)}) %collective-permute-start) | collective-permute-done | bytes 1179680 | tf_op jit(solution)/shard_map/while/body/eval_jaxpr/ppermute | solution.py:17
  576.5 5.2 fusion.48
  582.4 5.6 reduce-scatter.9.cloned.1.call-done
  588.0 132.1 %reduce-scatter.5.cloned.1.call-done = f32[96,2304]{1,0:T(8,128)} async-done(((f32[768,2304]{1,0:T(8,128)}), f32[96,2304]{1,0:T(8,128)}) %reduce-scatter.5.cloned.1.call-update) | async-done | bytes 884752 | tf_op jit(solution)/shard_map/reduce_scatter | solution.py:228
  720.1 5.5 fusion.41
  725.6 19.8 %all-reduce.4 = (f32[768]{0:T(1024)S(1)}, f32[768]{0:T(1024)S(1)}) all-reduce(f32[768]{0:T(1024)} %get-tuple-element.347, f32[768]{0:T(1024)S(1)} %copy-done.48), channel_id=3, replica_groups=mesh['fsdp'=8,'ctx'=4] {'fsdp'}, use_global_device_ids=true, to_apply=%region_14.15.clone | all-reduce | flops 1536 | bytes 12288
  745.6 6.1 all-reduce.5
  753.2 2.9 fusion.40
  757.8 22.9 %all-reduce.10.cloned.1.call-done = (f32[96,2304]{1,0:T(8,128)}, f32[96,768]{1,0:T(8,128)}, f32[96,2304]{1,0:T(8,128)}, f32[144,768]{1,0:T(8,128)}) async-done(((f32[96,2304]{1,0:T(8,128)}, f32[96,768]{1,0:T(8,128)}, f32[96,2304]{1,0:T(8,128)}, f32[144,768]{1,0:T(8,128)}), (f32[96,2304]{1,0:T(8,128)}, f32[96,768]{1,0:T(8,128)}, f32[96,2304]{1,0:T(8,128)}, ...) | async-done | bytes 2506768 | tf_op jit(solution)/shard_map/psum | solution.py:234
  (241 shorter events, 91.0 us)
Async XLA Ops:
  7.2 71.1 %copy-start.6 = (bf16[1,384,768]{2,1,0:T(8,128)(2,1)S(1)}, bf16[1,384,768]{2,1,0:T(8,128)(2,1)}, u32[]{:S(2)}) copy-start(bf16[1,384,768]{2,1,0:T(8,128)(2,1)} %param.12) | copy-start | bytes 1769476
  7.2 71.1 %all-gather.8.cloned.1.call-start = ((), (), s32[]{:S(2)}) async-start(), calls=%async_computation.4 | async-start | bytes 3981312 | tf_op jit(solution)/shard_map/all_gather | solution.py:105
  7.9 100.3 %all-gather.12.cloned.1.call-start = ((), (), s32[]{:S(2)}) async-start(), calls=%async_computation.6 | async-start | bytes 2949120 | tf_op jit(solution)/shard_map/all_gather | solution.py:132
  34.9 47.1 %copy-start.33 = (f32[768]{0:T(1024)}, f32[768]{0:T(1024)S(1)}, u32[]{:S(2)}) copy-start(f32[768]{0:T(1024)S(1)} %convert_element_type.98) | copy-start | bytes 9220
  36.8 45.1 %copy-start.36 = (f32[384]{0:T(512)}, f32[384]{0:T(512)S(1)}, u32[]{:S(2)}) copy-start(f32[384]{0:T(512)S(1)} %broadcast_multiply_fusion.6) | copy-start | bytes 4612
  38.2 43.8 %copy-start.38 = (f32[384]{0:T(512)}, f32[384]{0:T(512)S(1)}, u32[]{:S(2)}) copy-start(f32[384]{0:T(512)S(1)} %add_rsqrt_fusion.1) | copy-start | bytes 4612
  39.1 58.7 %copy-start.28 = (f32[384,32]{0,1:T(8,128)}, f32[384,32]{0,1:T(8,128)S(1)}, u32[]{:S(2)}) copy-start(f32[384,32]{0,1:T(8,128)S(1)} %get-tuple-element.405) | copy-start | bytes 147460
  85.5 4.0 copy-start.42
  85.5 48.9 %all-gather.10.cloned.1.call-start = ((), (), s32[]{:S(2)}) async-start(), calls=%async_computation.5 | async-start | bytes 2949120 | tf_op jit(solution)/shard_map/all_gather | solution.py:133
  87.7 89.9 %all-gather.14.cloned.1.call-start = ((), (), s32[]{:S(2)}) async-start(), calls=%async_computation.7 | async-start | bytes 1327104 | tf_op jit(solution)/shard_map/all_gather | solution.py:106
  88.3 155.4 %all-gather.16.cloned.1.call-start = ((), (), s32[]{:S(2)}) async-start(), calls=%async_computation.8 | async-start | bytes 3981312 | tf_op jit(solution)/shard_map/all_gather | solution.py:110
  88.9 201.3 %all-gather.18.cloned.1.call-start = ((), (), s32[]{:S(2)}) async-start(), calls=%async_computation.9 | async-start | bytes 1990656 | tf_op jit(solution)/shard_map/all_gather | solution.py:111
  89.5 492.9 %reduce-scatter.7.cloned.1.call-start = ((), (), s32[]{:S(2)}) async-start(), calls=%async_computation.11 | async-start | bytes 2654208 | tf_op jit(solution)/shard_map/reduce_scatter | solution.py:229
  98.0 10.2 %copy-start.22 = (bf16[384,12,32]{0,2,1:T(8,128)(2,1)}, bf16[384,12,32]{0,2,1:T(8,128)(2,1)S(1)}, u32[]{:S(2)}) copy-start(bf16[384,12,32]{0,2,1:T(8,128)(2,1)S(1)} %get-tuple-element.395) | copy-start | bytes 884740
  98.0 10.2 %copy-start.23 = (bf16[384,12,32]{0,2,1:T(8,128)(2,1)}, bf16[384,12,32]{0,2,1:T(8,128)(2,1)S(1)}, u32[]{:S(2)}) copy-start(bf16[384,12,32]{0,2,1:T(8,128)(2,1)S(1)} %get-tuple-element.396) | copy-start | bytes 884740
  98.0 10.2 %copy-start.30 = (pred[384,1536]{1,0:T(8,128)(4,1)S(1)}, pred[384,1536]{1,0:T(8,128)(4,1)}, u32[]{:S(2)}) copy-start(pred[384,1536]{1,0:T(8,128)(4,1)} %broadcast_compare_fusion.1) | copy-start | bytes 1769476
  123.5 15.2 %copy-start.40 = (f32[12,384]{1,0:T(8,128)}, f32[12,384]{1,0:T(8,128)S(1)}, u32[]{:S(2)}) copy-start(f32[12,384]{1,0:T(8,128)S(1)} %get-tuple-element.408) | copy-start | bytes 55300
  152.8 26.8 %copy-start.20 = (bf16[384,12,64]{0,2,1:T(8,128)(2,1)}, bf16[384,12,64]{0,2,1:T(8,128)(2,1)S(1)}, u32[]{:S(2)}) copy-start(bf16[384,12,64]{0,2,1:T(8,128)(2,1)S(1)} %get-tuple-element.410) | copy-start | bytes 1769476
  179.7 141.5 %copy-start.2 = (f32[384,768]{1,0:T(8,128)}, f32[384,768]{1,0:T(8,128)S(1)}, u32[]{:S(2)}) copy-start(f32[384,768]{1,0:T(8,128)S(1)} %get-tuple-element.413) | copy-start | bytes 3538948
  179.7 122.9 %copy-start.43 = (f32[384]{0:T(512)}, f32[384]{0:T(512)S(1)}, u32[]{:S(2)}) copy-start(f32[384]{0:T(512)S(1)} %broadcast_multiply_fusion.5) | copy-start | bytes 4612
  180.0 122.6 %copy-start.45 = (f32[384]{0:T(512)}, f32[384]{0:T(512)S(1)}, u32[]{:S(2)}) copy-start(f32[384]{0:T(512)S(1)} %add_rsqrt_fusion) | copy-start | bytes 4612
  180.0 110.2 %copy-start.18 = (bf16[1,384,768]{2,1,0:T(8,128)(2,1)S(1)}, bf16[1,384,768]{2,1,0:T(8,128)(2,1)}, u32[]{:S(2)}) copy-start(bf16[1,384,768]{2,1,0:T(8,128)(2,1)} %param.21) | copy-start | bytes 1769476
  290.2 7.2 copy-start.16
  297.8 4.8 copy-start.14
  297.8 8.1 %copy-start.9 = (bf16[384,1152]{1,0:T(8,128)(2,1)}, bf16[384,1152]{1,0:T(8,128)(2,1)S(1)}, u32[]{:S(2)}) copy-start(bf16[384,1152]{1,0:T(8,128)(2,1)S(1)} %get-tuple-element.388) | copy-start | bytes 2654212
  303.7 14.6 %copy-start.4 = (f32[384,768]{1,0:T(8,128)}, f32[384,768]{1,0:T(8,128)S(1)}, u32[]{:S(2)}) copy-start(f32[384,768]{1,0:T(8,128)S(1)} %multiply_add_fusion) | copy-start | bytes 3538948
  305.9 276.5 %reduce-scatter.11.cloned.1.call-start = ((), (), s32[]{:S(2)}) async-start(), calls=%async_computation.13 | async-start | bytes 3981312 | tf_op jit(solution)/shard_map/reduce_scatter | solution.py:232
  309.9 278.0 %reduce-scatter.9.cloned.1.call-start = ((), (), s32[]{:S(2)}) async-start(), calls=%async_computation.12 | async-start | bytes 7962624 | tf_op jit(solution)/shard_map/reduce_scatter | solution.py:231
  313.9 4.4 copy-start.13
  326.3 393.7 %reduce-scatter.5.cloned.1.call-start = ((), (), s32[]{:S(2)}) async-start(), calls=%async_computation.10 | async-start | bytes 7962624 | tf_op jit(solution)/shard_map/reduce_scatter | solution.py:228
  335.3 3.2 copy-start.8
  335.3 3.2 copy-start.47
  347.7 41.2 %collective-permute-start.1 = (f32[2,384,12,64]{1,3,2,0:T(8,128)}, f32[2,384,12,64]{1,3,2,0:T(8,128)}, u32[]{:S(2)}, u32[]{:S(2)}) collective-permute-start(f32[2,384,12,64]{1,3,2,0:T(8,128)} %maximum_add_fusion.2), channel_id=1, source_target_pairs={{0,1},{1,2},{2,3},{3,0},{4,5},{5,6},{6,7},{7,4},{8,9},{9,10},{10,1... | collective-permute-start | bytes 7077896 | tf_op jit(solution)/shard_map/while/body/eval_jaxpr/ppermute | solution.py:17
  347.7 41.2 %collective-permute-start = (bf16[2,384,768]{1,2,0:T(8,128)(2,1)}, bf16[2,384,768]{1,2,0:T(8,128)(2,1)}, u32[]{:S(2)}, u32[]{:S(2)}) collective-permute-start(bf16[2,384,768]{1,2,0:T(8,128)(2,1)} %copy.47), channel_id=1, source_target_pairs={{0,1},{1,2},{2,3},{3,0},{4,5},{5,6},{6,7},{7,4},{8,9},{9,10},{10,1... | collective-permute-start | bytes 3538952 | tf_op jit(solution)/shard_map/while/body/eval_jaxpr/ppermute | solution.py:17
  395.9 3.2 copy-start.8
  396.0 3.2 copy-start.47
  408.3 41.2 %collective-permute-start.1 = (f32[2,384,12,64]{1,3,2,0:T(8,128)}, f32[2,384,12,64]{1,3,2,0:T(8,128)}, u32[]{:S(2)}, u32[]{:S(2)}) collective-permute-start(f32[2,384,12,64]{1,3,2,0:T(8,128)} %maximum_add_fusion.2), channel_id=1, source_target_pairs={{0,1},{1,2},{2,3},{3,0},{4,5},{5,6},{6,7},{7,4},{8,9},{9,10},{10,1... | collective-permute-start | bytes 7077896 | tf_op jit(solution)/shard_map/while/body/eval_jaxpr/ppermute | solution.py:17
  408.3 41.2 %collective-permute-start = (bf16[2,384,768]{1,2,0:T(8,128)(2,1)}, bf16[2,384,768]{1,2,0:T(8,128)(2,1)}, u32[]{:S(2)}, u32[]{:S(2)}) collective-permute-start(bf16[2,384,768]{1,2,0:T(8,128)(2,1)} %copy.47), channel_id=1, source_target_pairs={{0,1},{1,2},{2,3},{3,0},{4,5},{5,6},{6,7},{7,4},{8,9},{9,10},{10,1... | collective-permute-start | bytes 3538952 | tf_op jit(solution)/shard_map/while/body/eval_jaxpr/ppermute | solution.py:17
  469.3 41.2 %collective-permute-start.1 = (f32[2,384,12,64]{1,3,2,0:T(8,128)}, f32[2,384,12,64]{1,3,2,0:T(8,128)}, u32[]{:S(2)}, u32[]{:S(2)}) collective-permute-start(f32[2,384,12,64]{1,3,2,0:T(8,128)} %maximum_add_fusion.2), channel_id=1, source_target_pairs={{0,1},{1,2},{2,3},{3,0},{4,5},{5,6},{6,7},{7,4},{8,9},{9,10},{10,1... | collective-permute-start | bytes 7077896 | tf_op jit(solution)/shard_map/while/body/eval_jaxpr/ppermute | solution.py:17
  469.3 41.2 %collective-permute-start = (bf16[2,384,768]{1,2,0:T(8,128)(2,1)}, bf16[2,384,768]{1,2,0:T(8,128)(2,1)}, u32[]{:S(2)}, u32[]{:S(2)}) collective-permute-start(bf16[2,384,768]{1,2,0:T(8,128)(2,1)} %copy.47), channel_id=1, source_target_pairs={{0,1},{1,2},{2,3},{3,0},{4,5},{5,6},{6,7},{7,4},{8,9},{9,10},{10,1... | collective-permute-start | bytes 3538952 | tf_op jit(solution)/shard_map/while/body/eval_jaxpr/ppermute | solution.py:17
  517.6 3.2 copy-start.8
  517.7 3.2 copy-start.47
  530.1 41.2 %collective-permute-start.1 = (f32[2,384,12,64]{1,3,2,0:T(8,128)}, f32[2,384,12,64]{1,3,2,0:T(8,128)}, u32[]{:S(2)}, u32[]{:S(2)}) collective-permute-start(f32[2,384,12,64]{1,3,2,0:T(8,128)} %maximum_add_fusion.2), channel_id=1, source_target_pairs={{0,1},{1,2},{2,3},{3,0},{4,5},{5,6},{6,7},{7,4},{8,9},{9,10},{10,1... | collective-permute-start | bytes 7077896 | tf_op jit(solution)/shard_map/while/body/eval_jaxpr/ppermute | solution.py:17
  530.1 41.2 %collective-permute-start = (bf16[2,384,768]{1,2,0:T(8,128)(2,1)}, bf16[2,384,768]{1,2,0:T(8,128)(2,1)}, u32[]{:S(2)}, u32[]{:S(2)}) collective-permute-start(bf16[2,384,768]{1,2,0:T(8,128)(2,1)} %copy.47), channel_id=1, source_target_pairs={{0,1},{1,2},{2,3},{3,0},{4,5},{5,6},{6,7},{7,4},{8,9},{9,10},{10,1... | collective-permute-start | bytes 3538952 | tf_op jit(solution)/shard_map/while/body/eval_jaxpr/ppermute | solution.py:17
  581.7 199.1 %all-reduce.10.cloned.1.call-start = ((), (), s32[]{:S(2)}) async-start(), calls=%async_computation.14 | async-start | bytes 5013504 | tf_op jit(solution)/shard_map/psum | solution.py:234
  720.1 5.6 copy-start.48
  720.1 33.1 %copy-start.5 = (f32[384,768]{1,0:T(8,128)S(1)}, f32[384,768]{1,0:T(8,128)}, u32[]{:S(2)}) copy-start(f32[384,768]{1,0:T(8,128)} %copy-done.4) | copy-start | bytes 3538948
  780.7 3.9 copy-start.31
  (31 other events, 62.0 us)
Sparse Core Ops, SparseCore 0:
  10.2 68.0 all-gather.7
  85.6 22.5 all-gather.11
  110.3 24.0 all-gather.9
  136.5 41.1 all-gather.13
  179.7 63.9 all-gather.15
  245.7 44.4 all-gather.17
  306.0 67.8 reduce-scatter.6
  377.5 78.1 reduce-scatter.10
  459.4 128.5 reduce-scatter.8
  592.0 128.0 reduce-scatter.4
  722.7 57.9 all-reduce.9
where the time goes:
time: 799 us; the launch traced here: 792 us
  waiting for transfers between devices  495 us (62%)
  matrix products  135 us (17%)
  blocking collectives  54.3 us (7%)
  local copies, waits for them, and re-layouts  50.7 us (6%)
  other arithmetic  34 us (4%)
  between operations  16.2 us (2%)
    ppermute x8, waiting for transfers between devices, from_behind(): lax.ppermute(shard, axis, [(i, (i + by) % count) for i in range(count)])  144 us
    reduce_scatter x1, waiting for transfers between devices, body(): lax.psum_scatter(grad_list[1], 'fsdp', scatter_dimension=0, tiled=True)  132 us
    all_gather x1, waiting for transfers between devices, body(): lax.all_gather(in_weight, 'fsdp', axis=0, tiled=True)  63.7 us
    unnamed x2, blocking collectives  43 us
    all_gather x1, waiting for transfers between devices, body(): lax.all_gather(down_weight, 'fsdp', axis=0, tiled=True)  41.1 us
    all_gather x1, waiting for transfers between devices, body(): lax.all_gather(qkv_weight, 'fsdp', axis=0, tiled=True)  39.2 us
    dot_general x6, matrix products, block_scores(): jnp.einsum('qhe,khe->hqk', split_heads(rows_low), split_heads(cols_low),...  25.9 us
    all_gather x1, waiting for transfers between devices, body(): lax.all_gather(out_weight, 'fsdp', axis=0, tiled=True)  24.8 us
  transfers between devices with their start and end apart: 19, of which 13 were waited for; matrix products, arithmetic and copies ran while one was open for 24% of the time, Pallas kernels for 0%

commit v1 on v0

v1 whole, which is shorter than its diff:
```python
import functools
import math

import jax
import jax.numpy as jnp
from jax import lax
from jax.experimental import pallas as pl
from jax.experimental.pallas import tpu as pltpu
from jax.sharding import PartitionSpec as P

HEAD_DIM = 64
rope_base = 160000.0
norm_eps = 1e-05
BF = jnp.bfloat16
F32 = jnp.float32
AXES = ("fsdp", "ctx")
EXP_SCALE = HEAD_DIM ** (-0.5) * math.log2(math.e)
MIB = 2**20


def nt(a, b):
    return lax.dot_general(a, b, (((1,), (1,)), ((), ())), preferred_element_type=F32)


def nn(a, b):
    return lax.dot_general(a, b, (((1,), (0,)), ((), ())), preferred_element_type=F32)


def tn(a, b):
    return lax.dot_general(a, b, (((0,), (0,)), ((), ())), preferred_element_type=F32)


def lanes(shape):
    return lax.broadcasted_iota(jnp.int32, shape, 1)


def split3(v):
    hi = v.astype(BF).astype(F32)
    rest = v - hi
    mid = rest.astype(BF).astype(F32)
    low = (rest - mid).astype(BF).astype(F32)
    return hi, mid, low


def swap_halves(u, lane):
    width = u.shape[1]
    return jnp.where((lane % 64) < 32, pltpu.roll(u, width - 32, 1), pltpu.roll(u, 32, 1))


def permute(x, fn, F, C):
    return lax.ppermute(x, AXES, [(i, fn(i)) for i in range(F * C)])


def flip_ctx(x, bit, F, C):
    return permute(x, lambda i: (i // C) * C + ((i % C) ^ bit), F, C)


def flip_fsdp(x, F, C):
    return permute(x, lambda i: (((i // C) ^ 1) * C) + i % C, F, C)


def ring(x, F, C):
    return permute(x, lambda i: (i + 2 * C) % (F * C), F, C)


def ctx_bits(C):
    bits = []
    b = C // 2
    while b:
        bits.append(b)
        b //= 2
    return bits


def gather_ctx(x, F, C):
    have = x[None]
    order = [0]
    for b in ctx_bits(C):
        have = jnp.concatenate([have, flip_ctx(have, b, F, C)], axis=0)
        order = order + [p ^ b for p in order]
    return have, order


def reduce_ctx(parts, F, C):
    for b in reversed(ctx_bits(C)):
        half = parts.shape[0] // 2
        got = flip_ctx(parts[half:].astype(BF), b, F, C)
        parts = parts[:half] + got.astype(F32)
    return parts[0]


def reduce_steps(grads, F, C):
    core = lax.axis_index("ctx") % 2
    keep_parts, give_parts = [], []
    for g in grads:
        g3 = g.astype(BF).reshape(F, g.shape[0] // F, g.shape[1])
        half = g.shape[1] // 2
        for j in range(0, half, 384):
            a = g3[:, :, j : j + 384]
            b = g3[:, :, half + j : half + j + 384]
            keep_parts.append(jnp.where(core == 0, a, b))
            give_parts.append(jnp.where(core == 0, b, a))
    give = jnp.concatenate(give_parts, axis=1)
    keep = jnp.concatenate(keep_parts, axis=1)
    yield give
    got = flip_ctx(give, 1, F, C)
    acc = (keep.astype(F32) + got.astype(F32)).astype(BF)
    yield acc
    Z = F // 2
    me = lax.axis_index("fsdp")
    z, xx = me // 2, me % 2
    total = None
    for s in range(Z):
        d = lax.rem(z - 1 - s + Z, Z)
        got = flip_fsdp(lax.dynamic_index_in_dim(acc, d * 2 + 1 - xx, 0, False), F, C)
        mine = lax.dynamic_index_in_dim(acc, d * 2 + xx, 0, False).astype(F32) + got.astype(F32)
        total = mine if total is None else mine + arrived.astype(F32)
        if s < Z - 1:
            send = total.astype(BF)
            yield send
            arrived = ring(send, F, C)
    for b in ctx_bits(C)[:-1]:
        total = total + flip_ctx(total.astype(BF), b, F, C).astype(F32)
    other = flip_ctx(total.astype(BF), 1, F, C).astype(F32)
    first = jnp.where(core == 0, total, other)
    second = jnp.where(core == 0, other, total)
    outs = []
    row = 0
    for g in grads:
        n, count = g.shape[0] // F, g.shape[1] // 768
        cols = [side[row + j * n : row + (j + 1) * n] for side in (first, second) for j in range(count)]
        row += n * count
        outs.append(jnp.concatenate(cols, axis=1))
    yield outs


def finish(steps):
    for last in steps:
        pass
    return last


def unpack_kernel(idx_ref, own_ref, got_ref, *refs, F, places):
    outs, sems = refs[:-1], refs[-1]
    piece = own_ref.shape[0] // F
    copies = []
    for j in range(F):
        for side, src in ((0, own_ref), (1, got_ref)):
            for row, n, o, half, col in places:
                r = pl.multiple_of(idx_ref[j] * n, n)
                c = pl.multiple_of(idx_ref[F + side] * half + col, 128)
                copies.append(
                    pltpu.make_async_copy(
                        src.at[pl.ds(j * piece + row, n), :],
                        outs[o].at[pl.ds(r, n), pl.ds(c, src.shape[1])],
                        sems.at[len(copies)],
                    )
                )
    for c in copies:
        c.start()
    for c in copies:
        c.wait()


def unpack(own, got, idx, F, places, shapes):
    return pl.pallas_call(
        functools.partial(unpack_kernel, F=F, places=places),
        in_specs=[
            pl.BlockSpec(memory_space=pltpu.SMEM),
            pl.BlockSpec(memory_space=pl.ANY),
            pl.BlockSpec(memory_space=pl.ANY),
        ],
        out_specs=[pl.BlockSpec(memory_space=pltpu.VMEM)] * len(shapes),
        out_shape=[jax.ShapeDtypeStruct(s, own.dtype) for s in shapes],
        scratch_shapes=[pltpu.SemaphoreType.DMA((2 * F * len(places),))],
        compiler_params=pltpu.CompilerParams(vmem_limit_bytes=32 * MIB),
        name="unpack",
    )(idx, own, got)


def project_kernel(idx_ref, x_ref, gain_ref, own_ref, got_ref, cos_ref, sin_ref, h_ref, q_ref, k_ref, v_ref, w_ref, sems, *, F, n):
    rows, width = h_ref.shape
    half = w_ref.shape[1] // 2
    piece = own_ref.shape[0] // F

    def copies():
        made = []
        for j in range(F):
            for side, src in ((0, own_ref), (1, got_ref)):
                r = pl.multiple_of(idx_ref[j] * n, n)
                c = pl.multiple_of(idx_ref[F + side] * half, 128)
                made.append(
                    pltpu.make_async_copy(
                        src.at[pl.ds(j * piece, n), :], w_ref.at[pl.ds(r, n), pl.ds(c, half)], sems.at[len(made)]
                    )
                )
        return made

    @pl.when(pl.program_id(0) == 0)
    def _():
        made = copies()
        for c in made:
            c.start()
        for c in made:
            c.wait()

    x = x_ref[0, :rows, :].astype(F32)
    centred = x - jnp.mean(x, axis=1, keepdims=True)
    var = jnp.mean(centred * centred, axis=1, keepdims=True)
    h = (centred * lax.rsqrt(var + norm_eps) * gain_ref[...]).astype(BF)
    h_ref[...] = h
    cos, sin = cos_ref[...], sin_ref[...]
    lane = lanes((rows, 128))

    def rope_into(ref, offset):
        for j in range(0, width, 256):
            u = nn(h, w_ref[:, offset + j : offset + j + 256])
            for i in (0, 128):
                t = u[:, i : i + 128]
                ref[:, j + i : j + i + 128] = (t * cos + swap_halves(t, lane) * sin).astype(BF)

    rope_into(k_ref, width)
    for j in range(0, width, 256):
        v_ref[:, j : j + 256] = nn(h, w_ref[:, 2 * width + j : 2 * width + j + 256]).astype(BF)

    @pl.when(pl.program_id(0) == 0)
    def _():
        rope_into(q_ref, 0)


def project(xs, gain, own, got, idx, cos, sin, rows, F):
    C, _, width = xs.shape
    blk = pl.BlockSpec((rows, width), lambda i: (i, 0))
    tab = pl.BlockSpec((rows, 128), lambda i: (i, 0))
    whole = lambda i: (0, 0)
    out = jax.ShapeDtypeStruct((C * rows, width), BF)
    return pl.pallas_call(
        functools.partial(project_kernel, F=F, n=width // F),
        grid=(C,),
        in_specs=[
            pl.BlockSpec(memory_space=pltpu.SMEM),
            pl.BlockSpec((1,) + xs.shape[1:], lambda i: (i, 0, 0)),
            pl.BlockSpec((1, width), whole),
            pl.BlockSpec(memory_space=pl.ANY),
            pl.BlockSpec(memory_space=pl.ANY),
            tab,
            tab,
        ],
        out_specs=[blk, pl.BlockSpec((rows, width), whole), blk, blk, pl.BlockSpec((width, 3 * width), whole)],
        out_shape=[out, jax.ShapeDtypeStruct((rows, width), BF), out, out, jax.ShapeDtypeStruct((width, 3 * width), BF)],
        scratch_shapes=[pltpu.SemaphoreType.DMA((2 * F,))],
        compiler_params=pltpu.CompilerParams(vmem_limit_bytes=40 * MIB),
        name="project",
    )(idx, xs, gain, own, got, cos, sin)


def forward_kernel(q_ref, k_ref, v_ref, f_ref, fq_ref, after_ref, mix_ref, low_ref, m_ref, t_ref, *, rows, blocks):
    low = lanes((rows, 128)) < 64
    q, fq = q_ref[...], fq_ref[...]
    outs = []
    for x in range(2):
        pick = low if x == 0 else ~low
        qx = jnp.where(pick, q, fq)
        acc = None
        for j in range(blocks):
            sl = pl.ds(j * rows, rows)
            f = f_ref[sl, :]
            kx = jnp.where(pick, k_ref[sl, :], f)
            vx = jnp.where(pick, v_ref[sl, :], f)
            s = nt(qx, kx)
            if j == 0:
                top = jnp.max(s, axis=1, keepdims=True)
            p = jnp.exp2((s - top) * EXP_SCALE).astype(BF)
            a = nn(p, vx)
            acc = a if acc is None else acc + a
        at = 70 if x == 0 else 6
        tot = acc[:, at : at + 1]
        outs.append((acc / tot, top, tot))
    (a0, m0, t0), (a1, m1, t1) = outs
    mix = jnp.where(low, a0, a1)
    mix_ref[...] = mix
    low_ref[...] = mix.astype(BF)
    m_ref[...] = jnp.where(low, m1, m0)
    t_ref[...] = jnp.where(low, t0, t1)


def attend(q, k, v, f, fq, after, first, n):
    rows, T = q.shape[0], k.shape[0]
    qs = pl.BlockSpec((rows, 128), lambda i: (0, i + first))
    ks = pl.BlockSpec((T, 128), lambda i: (0, i + first))
    cf = pl.BlockSpec((T, 128), lambda i: (0, 0))
    cq = pl.BlockSpec((rows, 128), lambda i: (0, 0))
    oq = pl.BlockSpec((rows, 128), lambda i: (0, i))
    out = jax.ShapeDtypeStruct((rows, 128 * n), F32)
    return pl.pallas_call(
        functools.partial(forward_kernel, rows=rows, blocks=T // rows),
        grid=(n,),
        in_specs=[qs, ks, ks, cf, cq, pl.BlockSpec(memory_space=pl.ANY)],
        out_specs=[oq] * 4,
        out_shape=[out, jax.ShapeDtypeStruct((rows, 128 * n), BF), out, out],
        compiler_params=pltpu.CompilerParams(vmem_limit_bytes=40 * MIB),
        name="attend",
    )(q, k, v, f, fq, after)


def backward_kernel(
    q_ref, k_ref, v_ref, f_ref, fq_ref, m_ref, t_ref, mix_ref, gm_ref, cos_ref, sin_ref, after_ref,
    dq_ref, dk_ref, dv_ref, sk_ref, sv_ref, *, rows, blocks,
):
    lane = lanes((rows, 128))
    low = lane < 64
    slot = lane % 64
    q = q_ref[...]
    ga = gm_ref[...] / t_ref[...]
    prod = ga * mix_ref[...]
    hi, mid, lo = split3(m_ref[...])
    fq = jnp.where(slot == 3, -hi, jnp.where(slot == 4, -mid, jnp.where(slot == 5, -lo, fq_ref[...].astype(F32)))).astype(BF)
    gab = ga.astype(BF)
    dqs = []
    for x in range(2):
        pick = low if x == 0 else ~low
        qx = jnp.where(pick, q, fq)
        delta = jnp.sum(jnp.where(pick, prod, 0.0), axis=1, keepdims=True)
        h3, m3, l3 = split3(jnp.broadcast_to(delta, (rows, 128)))
        gf = jnp.where(slot == 6, -h3, jnp.where(slot == 7, -m3, jnp.where(slot == 8, -l3, 0.0))).astype(BF)
        gx = jnp.where(pick, gab, gf)
        gxt = gx.T[64 * x : 64 * x + 64]
        qxt = qx.T[64 * x : 64 * x + 64]
        dq = None
        for j in range(blocks):
            sl = pl.ds(j * rows, rows)
            f = f_ref[sl, :]
            kx = jnp.where(pick, k_ref[sl, :], f)
            vx = jnp.where(pick, v_ref[sl, :], f)
            p = jnp.exp2(nt(qx, kx) * EXP_SCALE)
            ds = (p * nt(gx, vx)).astype(BF)
            d = nn(ds, kx)
            dq = d if dq is None else dq + d
            sv_ref[64 * x : 64 * x + 64, sl] = nn(gxt, p.astype(BF))
            sk_ref[64 * x : 64 * x + 64, sl] = nn(qxt, ds)
        dqs.append(dq)
    scale = HEAD_DIM ** (-0.5)

    def unrope(u, sl):
        return (u * cos_ref[sl, :] - swap_halves(u, lane) * sin_ref[sl, :]).astype(BF)

    dq_ref[...] = unrope(jnp.where(low, dqs[0], dqs[1]) * scale, pl.ds(0, rows))
    for j in range(blocks):
        sl = pl.ds(j * rows, rows)
        dv_ref[sl, :] = sv_ref[:, sl].T.astype(BF)
        dk_ref[sl, :] = unrope(sk_ref[:, sl].T * scale, sl)


def attend_back(q, k, v, f, fq, top, tot, mix, gm, cos, sin, after, first, n):
    rows, T = q.shape[0], k.shape[0]
    qs = pl.BlockSpec((rows, 128), lambda i: (0, i + first))
    ks = pl.BlockSpec((T, 128), lambda i: (0, i + first))
    cf = pl.BlockSpec((T, 128), lambda i: (0, 0))
    cq = pl.BlockSpec((rows, 128), lambda i: (0, 0))
    oq = pl.BlockSpec((rows, 128), lambda i: (0, i))
    ok = pl.BlockSpec((T, 128), lambda i: (0, i))
    return pl.pallas_call(
        functools.partial(backward_kernel, rows=rows, blocks=T // rows),
        grid=(n,),
        in_specs=[qs, ks, ks, cf, cq, oq, oq, oq, qs, cf, cf, pl.BlockSpec(memory_space=pl.ANY)],
        out_specs=[oq, ok, ok],
        out_shape=[jax.ShapeDtypeStruct((rows, 128 * n), BF)] + [jax.ShapeDtypeStruct((T, 128 * n), BF)] * 2,
        scratch_shapes=[pltpu.VMEM((128, T), F32), pltpu.VMEM((128, T), F32)],
        compiler_params=pltpu.CompilerParams(vmem_limit_bytes=48 * MIB),
        name="attend_back",
    )(q, k, v, f, fq, top, tot, mix, gm, cos, sin, after)


def normalize(fields):
    centred = fields - jnp.mean(fields, axis=-1, keepdims=True)
    variance = jnp.mean(centred * centred, axis=-1, keepdims=True)
    inv_root = lax.rsqrt(variance + norm_eps)
    return centred * inv_root, inv_root


def norm_back(grad_out, normed, inv_root, gain):
    scaled = grad_out * gain
    return inv_root * (
        scaled
        - jnp.mean(scaled, axis=-1, keepdims=True)
        - normed * jnp.mean(scaled * normed, axis=-1, keepdims=True)
    )


def tables(docs, places):
    lane = jnp.arange(128)
    frequency = rope_base ** (-2.0 * (lane % 32).astype(F32) / HEAD_DIM)
    angles = places.astype(F32)[:, None] * frequency[None, :]
    sign = jnp.where(lane % 64 < 32, -1.0, 1.0)
    slot = lane % 64
    same = (docs[:, None] == slot[None, :]) & (slot < 3)[None, :]
    ones = ((slot >= 3) & (slot < 9))[None, :]
    feats = jnp.where(same | ones, 1.0, 0.0).astype(BF)
    return jnp.cos(angles), jnp.sin(angles) * sign, feats


def core_half(shard, core):
    half = shard.shape[1] // 2
    return lax.dynamic_slice_in_dim(shard, core * half, half, 1)


def gather_steps(piece, F, C):
    Z = F // 2
    same = piece
    for k in range(Z):
        other = flip_fsdp(same, F, C)
        nxt = ring(same, F, C) if k < Z - 1 else None
        yield same, other
        same = nxt


def owners_of(F):
    Z = F // 2
    me = lax.axis_index("fsdp")
    z, xx = me // 2, me % 2
    owners = []
    for k in range(Z):
        base = lax.rem(z - k + Z, Z) * 2
        owners += [base + xx, base + 1 - xx]
    return owners


def both_cores(pieces, F, C):
    own = jnp.concatenate(pieces, axis=0)
    return own, flip_ctx(own, 1, F, C)


def body(
    F, C, hidden_in, segment_ids, positions, norm1_gain, qkv_weight, out_weight, norm2_gain, in_weight, down_weight, out_cot
):
    width = hidden_in.shape[-1]
    rows = hidden_in.shape[1]
    inputs = hidden_in.reshape(rows, width)
    docs = segment_ids.reshape(-1)
    places = positions.reshape(-1)
    extra = jnp.zeros((16, width), BF)
    meta = jnp.stack([docs, places // 256, places % 256]).astype(BF)
    extra = lax.dynamic_update_slice(extra, meta, (0, 0))
    xs, _ = gather_ctx(jnp.concatenate([inputs, extra], axis=0), F, C)
    core = lax.axis_index("ctx") % 2
    owners = owners_of(F)
    idx = jnp.stack([jnp.asarray(o, jnp.int32) for o in owners] + [core, 1 - core]).astype(jnp.int32)
    n = width // F
    half = core_half(qkv_weight, core)
    gain_rows = lax.dynamic_update_slice(
        jnp.zeros((16, half.shape[1]), BF), jnp.concatenate([norm1_gain, norm2_gain])[None], (0, 0)
    )
    pieces = [p for step in gather_steps(jnp.concatenate([half, gain_rows], axis=0), F, C) for p in step]
    own_a, got_a = both_cores(pieces, F, C)
    gain_pieces = own_a.reshape(F, n + 16, -1)[:, n, : 2 * n].astype(F32)
    place = jnp.stack(owners)[None, :] == jnp.arange(F)[:, None]
    gains = jnp.sum(jnp.where(place[:, :, None], gain_pieces[None], 0.0), axis=1).reshape(F, 2, n)
    gain_one, gain_two = gains[:, 0].reshape(1, width), gains[:, 1].reshape(1, width)

    all_meta = xs[:, rows : rows + 3, :rows].astype(jnp.int32)
    all_docs = all_meta[:, 0].reshape(-1)
    all_places = (all_meta[:, 1] * 256 + all_meta[:, 2]).reshape(-1)
    cos, sin, feats = tables(all_docs, all_places)
    slot = jnp.arange(128) % 64
    query_feats = jnp.where((slot < 3)[None, :] & (docs[:, None] != slot[None, :]), -1e30, 0.0).astype(BF)

    n_down = down_weight.shape[0]
    ring_b = n_down % 16 == 0
    if ring_b:
        wide = core_half(in_weight, core)
        parts_b = [core_half(out_weight, core)] + [wide[:, j : j + 384] for j in range(0, wide.shape[1], 384)]
        piece_b = jnp.concatenate(parts_b + [core_half(down_weight, core)], axis=0)
        piece_b, _ = lax.optimization_barrier((piece_b, pieces[-1]))
        steps_b = list(gather_steps(piece_b, F, C))
    else:
        steps_b = []
    h_all, query, key, value, w_qkv = project(xs, gain_one, own_a, got_a, idx, cos, sin, rows, F)
    pairs = width // 128
    calls = 3
    per = pairs // calls
    ahead = [
        attend(query, key, value, feats, query_feats, steps_b[i + 1][0] if i + 1 < len(steps_b) else query_feats, i * per, per)
        for i in range(calls)
    ]
    mixed_low = jnp.concatenate([a[1] for a in ahead], axis=1)
    if ring_b:
        own_b, got_b = both_cores([p for step in steps_b for p in step], F, C)
        places = [(0, n, 0, 384, 0)]
        places += [(n * (1 + j), n, 1, wide.shape[1], 384 * j) for j in range(wide.shape[1] // 384)]
        places += [(piece_b.shape[0] - n_down, n_down, 2, 384, 0)]
        shapes = [(width, width), (width, in_weight.shape[1]), (n_down * F, width)]
        w_out, w_in, w_down = unpack(own_b, got_b, idx, F, places, shapes)
    else:
        w_out, w_in, w_down = [
            lax.all_gather(w, "fsdp", axis=0, tiled=True) for w in (out_weight, in_weight, down_weight)
        ]

    resid_in = inputs.astype(F32)
    resid = resid_in + nn(mixed_low, w_out)
    normed_two, inv_two = normalize(resid)
    h_two = (normed_two * gain_two).astype(BF)
    ff = w_down.shape[0]
    up_all = nn(h_two, w_in)
    gate, up = up_all[:, :ff], up_all[:, ff:]
    cdf = 0.5 * (1.0 + lax.erf(gate * math.sqrt(0.5)))
    pdf = jnp.exp(-0.5 * gate * gate) * (1.0 / math.sqrt(2.0 * math.pi))
    gelu = gate * cdf
    mid = (gelu * up).astype(BF)
    out = (resid + nn(mid, w_down)).astype(BF).reshape(hidden_in.shape)
    branch = out_cot.reshape(rows, width)
    grad_down = tn(mid, branch)
    grad_mid = nt(branch, w_down)
    grad_u = jnp.concatenate([grad_mid * up * (cdf + gate * pdf), grad_mid * gelu], axis=1).astype(BF)
    grad_in = tn(h_two, grad_u)
    grad_h_two = nt(grad_u, w_in)
    grad_resid = branch.astype(F32) + norm_back(grad_h_two, normed_two, inv_two, gain_two)
    grad_attn = grad_resid.astype(BF)
    grad_out = tn(mixed_low, grad_attn)
    grad_mixed = nt(grad_attn, w_out)

    sum_b = reduce_steps([grad_down, grad_in, grad_out], F, C)
    marks = [next(sum_b) for _ in range(calls)]
    parts = [
        attend_back(
            query, key, value, feats, query_feats, ahead[i][2], ahead[i][3], ahead[i][0], grad_mixed, cos, sin,
            marks[i], i * per, per,
        )
        for i in range(calls)
    ]
    g_down, g_in, g_out = finish(sum_b)
    g_query = jnp.concatenate([p[0] for p in parts], axis=1)
    g_kv = jnp.concatenate([p[1] for p in parts] + [p[2] for p in parts], axis=1)
    h_own = h_all[:rows]
    grad_qkv = jnp.concatenate([tn(h_own, g_query), tn(h_all, g_kv)], axis=1)
    (g_qkv,) = finish(reduce_steps([grad_qkv], F, C))
    grad_h = nt(g_kv, w_qkv[:, width:]).reshape(C, rows, width)
    own_h = nt(g_query, w_qkv[:, :width])
    grad_h_one = reduce_ctx(grad_h, F, C) + own_h
    normed_one, inv_one = normalize(resid_in)
    in_grad = (grad_resid + norm_back(grad_h_one, normed_one, inv_one, gain_one)).reshape(hidden_in.shape)
    g_gain_one = jnp.sum(g_qkv * qkv_weight.astype(F32), axis=1) / norm1_gain.astype(F32)
    g_gain_two = jnp.sum(g_in * in_weight.astype(F32), axis=1) / norm2_gain.astype(F32)
    return (out, in_grad, g_gain_one, g_qkv, g_out, g_gain_two, g_in, g_down)


def solution(mesh):
    F, C = mesh.shape["fsdp"], mesh.shape["ctx"]
    tokens = P("fsdp", "ctx", None)
    ids = P("fsdp", "ctx")
    vec = P("fsdp")
    mat = P("fsdp", None)
    return jax.shard_map(
        functools.partial(body, F, C),
        mesh=mesh,
        in_specs=(tokens, ids, ids, vec, mat, mat, vec, mat, mat, tokens),
        out_specs=(tokens, tokens, vec, mat, mat, vec, mat, mat),
        check_vma=False,
    )
```

time: 799 us -> 313 us (0.39)
  waiting for transfers between devices: 495 us -> 127 us
  matrix products: 135 us -> 27.3 us
  Pallas kernels: 0 us -> 56 us
  blocking collectives: 54.3 us -> 0 us
  starting transfers between devices: 6.2 us -> 25.6 us
  local copies, waits for them, and re-layouts: 50.7 us -> 35.6 us
  between operations: 16.2 us -> 2.34 us
    all_gather x6 -> x0, waiting for transfers between devices: 188 us -> none  [the longest x1 63.7 us: body(): lax.all_gather(in_weight, 'fsdp', axis=0, tiled=True)]
    reduce_scatter x4 -> x0, waiting for transfers between devices: 138 us -> none  [the longest x1 132 us: body(): lax.psum_scatter(grad_list[1], 'fsdp', scatter_dimension=0, tiled=True)]
    dot_general x35 -> x13, matrix products: 135 us -> 27.3 us  [the longest x5 14 us: nt(): lax.dot_general(a, b, (((1,), (1,)), ((), ())), preferred_element_type=F32)]
    pallas_call x0 -> x8, Pallas kernels: none -> 56 us  [the longest x3 27.2 us: attend_back(): pl.pallas_call(functools.partial(backward_kernel, rows=rows, blocks=T //...]
    unnamed x2 -> x0, blocking collectives: 43 us -> none
    psum x1 -> x0, waiting for transfers between devices: 22.9 us -> none  [body(): lax.psum((shares[0], shares[1], shares[2], shares[3], shares[4], shares[5...]
    ppermute x8 -> x40, starting transfers between devices: 5.76 us -> 25.6 us  [permute(): return lax.ppermute(x, AXES, [(i, fn(i)) for i in range(F * C)])]
    ppermute x8 -> x40, waiting for transfers between devices: 144 us -> 127 us  [permute(): return lax.ppermute(x, AXES, [(i, fn(i)) for i in range(F * C)])]
  transfers between devices with their start and end apart: 19 -> 40, of which waited for: 13 -> 23; matrix products, arithmetic and copies ran while one was open for 24% -> 19% of each run, Pallas kernels for 0% -> 17%
where the time goes in v1:
time: 313 us; the launch traced here: 308 us
  waiting for transfers between devices  127 us (41%)
  Pallas kernels  56 us (18%)
  local copies, waits for them, and re-layouts  35.6 us (11%)
  other arithmetic  34.2 us (11%)
  matrix products  27.3 us (9%)
  starting transfers between devices  25.6 us (8%)
    ppermute x40, waiting for transfers between devices, permute(): return lax.ppermute(x, AXES, [(i, fn(i)) for i in range(F * C)])  127 us
    unnamed x162, local copies, waits for them, and re-layouts  30.2 us
    pallas_call x3, Pallas kernels, attend_back(): pl.pallas_call(functools.partial(backward_kernel, rows=rows, blocks=T //...  27.2 us
    ppermute x40, starting transfers between devices, permute(): return lax.ppermute(x, AXES, [(i, fn(i)) for i in range(F * C)])  25.6 us
    dot_general x5, matrix products, nt(): lax.dot_general(a, b, (((1,), (1,)), ((), ())), preferred_element_type=F32)  14 us
    pallas_call x3, Pallas kernels, attend(): pl.pallas_call(functools.partial(forward_kernel, rows=rows, blocks=T // r...  13.2 us
    pallas_call x1, Pallas kernels, project(): pl.pallas_call(functools.partial(project_kernel, F=F, n=width // F), grid...  11.4 us
    dot_general x5, matrix products, tn(): lax.dot_general(a, b, (((0,), (0,)), ((), ())), preferred_element_type=F32)  9.28 us
  transfers between devices with their start and end apart: 40, of which 23 were waited for; matrix products, arithmetic and copies ran while one was open for 19% of the time, Pallas kernels for 17%

profile of v1, /device:TPU:0, one launch (start us, length us, event | category | flops | bytes accessed | tf_op | source)
XLA Modules:
  0.0 307.8 jit_solution(15218601753665426379)
XLA Ops:
  3.2 2.9 collective-permute-start.2
  9.2 1.9 maximum_bitcast_fusion
  13.3 2.6 collective-permute-done.3
  17.3 7.4 %collective-permute-done.5 = bf16[112,1152]{1,0:T(8,128)(2,1)} collective-permute-done((bf16[112,1152]{1,0:T(8,128)(2,1)S(1)}, bf16[112,1152]{1,0:T(8,128)(2,1)}, u32[]{:S(2)}, u32[]{:S(2)}) %collective-permute-start.5) | collective-permute-done | bytes 258080 | tf_op jit(solution)/shard_map/ppermute | solution.py:51
  24.8 8.2 %collective-permute-done.7 = bf16[112,1152]{1,0:T(8,128)(2,1)S(1)} collective-permute-done((bf16[112,1152]{1,0:T(8,128)(2,1)}, bf16[112,1152]{1,0:T(8,128)(2,1)S(1)}, u32[]{:S(2)}, u32[]{:S(2)}) %collective-permute-start.7) | collective-permute-done | bytes 258080 | tf_op jit(solution)/shard_map/ppermute | solution.py:51
  35.9 5.1 %collective-permute-done.8 = bf16[112,1152]{1,0:T(8,128)(2,1)S(1)} collective-permute-done((bf16[112,1152]{1,0:T(8,128)(2,1)S(1)}, bf16[112,1152]{1,0:T(8,128)(2,1)S(1)}, u32[]{:S(2)}, u32[]{:S(2)}) %collective-permute-start.8) | collective-permute-done | bytes 258080 | tf_op jit(solution)/shard_map/ppermute | solution.py:51
  42.5 11.1 %collective-permute-done.10.after_ref = bf16[528,384]{1,0:T(8,128)(2,1)S(1)} collective-permute-done((bf16[528,384]{1,0:T(8,128)(2,1)}, bf16[528,384]{1,0:T(8,128)(2,1)S(1)}, u32[]{:S(2)}, u32[]{:S(2)}) %collective-permute-start.10) | collective-permute-done | bytes 405536 | tf_op jit(solution)/shard_map/ppermute | solution.py:51
  54.7 2.0 collective-permute-start.13
  56.8 10.4 %collective-permute-done.11.after_ref = bf16[528,384]{1,0:T(8,128)(2,1)S(1)} collective-permute-done((bf16[528,384]{1,0:T(8,128)(2,1)S(1)}, bf16[528,384]{1,0:T(8,128)(2,1)S(1)}, u32[]{:S(2)}, u32[]{:S(2)}) %collective-permute-start.11) | collective-permute-done | bytes 405536 | tf_op jit(solution)/shard_map/ppermute | solution.py:51
  68.4 1.8 constant_dynamic-update-slice_fusion.24
  74.0 2.9 collective-permute-done.12.after_ref
  76.9 2.2 collective-permute-done.14
  80.7 2.8 collective-permute-done.15
  85.1 2.7 collective-permute-done.16
  88.7 2.4 pad_maximum_fusion.3
  93.3 5.0 %collective-permute-done.1 = bf16[2,400,768]{2,1,0:T(8,128)(2,1)} collective-permute-done((bf16[2,400,768]{2,1,0:T(8,128)(2,1)}, bf16[2,400,768]{2,1,0:T(8,128)(2,1)}, u32[]{:S(2)}, u32[]{:S(2)}) %collective-permute-start.1) | collective-permute-done | bytes 1228832 | tf_op jit(solution)/shard_map/ppermute | solution.py:51
  98.3 1.9 pad_maximum_fusion.x_ref
  102.0 2.8 fusion.33
  105.5 11.4 %project.1 = (bf16[1536,768]{1,0:T(8,128)(2,1)S(1)}, bf16[384,768]{1,0:T(8,128)(2,1)S(1)}, bf16[1536,768]{1,0:T(8,128)(2,1)S(1)}, bf16[1536,768]{1,0:T(8,128)(2,1)S(1)}, bf16[768,2304]{1,0:T(8,128)(2,1)}) custom-call(s32[10]{0:T(128)S(1)} %copy-done.25, bf16[4,400,768]{2,1,0:T(8,128)(2,1)} %copy-done.39, f32[1,768]{1,0:T(1,128)S(1)} %reshape_squeeze.4.gain_ref, ...), custom_call_target="tpu_custom_call" | custom-call | tf_op jit(solution)/shard_map/project/pallas_call | solution.py:237
  118.4 4.4 %attend.3 = (f32[384,256]{1,0:T(8,128)S(1)}, bf16[384,256]{1,0:T(8,128)(2,1)S(1)}, f32[384,256]{1,0:T(8,128)S(1)}, f32[384,256]{1,0:T(8,128)S(1)}) custom-call(bf16[384,768]{1,0:T(8,128)(2,1)S(1)} %get-tuple-element.38.q_ref, bf16[1536,768]{1,0:T(8,128)(2,1)S(1)} %get-tuple-element.39.k_ref, bf16[1536,768]{1,0:T(8,128)(2,1)S(1)} %get-tuple-element.40.v_ref, ...), custom_call_target="tpu_custom_call" | custom-call | tf_op jit(solution)/shard_map/attend/pallas_call | solution.py:295
  125.1 4.4 %attend.4 = (f32[384,256]{1,0:T(8,128)S(1)}, bf16[384,256]{1,0:T(8,128)(2,1)S(1)}, f32[384,256]{1,0:T(8,128)S(1)}, f32[384,256]{1,0:T(8,128)S(1)}) custom-call(bf16[384,768]{1,0:T(8,128)(2,1)S(1)} %get-tuple-element.38.q_ref, bf16[1536,768]{1,0:T(8,128)(2,1)S(1)} %get-tuple-element.39.k_ref, bf16[1536,768]{1,0:T(8,128)(2,1)S(1)} %get-tuple-element.40.v_ref, ...), custom_call_target="tpu_custom_call" | custom-call | tf_op jit(solution)/shard_map/attend/pallas_call | solution.py:295
  130.3 4.4 %attend.5 = (f32[384,256]{1,0:T(8,128)S(1)}, bf16[384,256]{1,0:T(8,128)(2,1)S(1)}, f32[384,256]{1,0:T(8,128)S(1)}, f32[384,256]{1,0:T(8,128)S(1)}) custom-call(bf16[384,768]{1,0:T(8,128)(2,1)S(1)} %get-tuple-element.38.q_ref, bf16[1536,768]{1,0:T(8,128)(2,1)S(1)} %get-tuple-element.39.k_ref, bf16[1536,768]{1,0:T(8,128)(2,1)S(1)} %get-tuple-element.40.v_ref, ...), custom_call_target="tpu_custom_call" | custom-call | tf_op jit(solution)/shard_map/attend/pallas_call | solution.py:295
  134.8 4.2 %unpack.1 = (bf16[768,768]{1,0:T(8,128)(2,1)S(1)}, bf16[768,2304]{1,0:T(8,128)(2,1)S(1)}, bf16[1152,768]{1,0:T(8,128)(2,1)S(1)}) custom-call(s32[10]{0:T(128)S(1)} %copy-done.25, bf16[4224,384]{1,0:T(8,128)(2,1)} %constant_dynamic-update-slice_fusion.17.own_ref, bf16[4224,384]{1,0:T(8,128)(2,1)} %collective-permute-done.17.got_ref), custom_call_target="tpu_custom_call" | custom-call | tf_op jit(solution)/shard_map/unpack/pallas_call | solution.py:166
  140.1 1.6 fusion.66
  141.8 1.9 fusion.7
  143.7 1.7 fusion.68
  145.4 2.2 convolution_convert_fusion
  150.0 1.6 select_dynamic-update-slice_fusion
  159.4 3.5 %fusion.45.gm_ref = f32[384,768]{1,0:T(8,128)} fusion(bf16[768,768]{1,0:T(8,128)(2,1)} %copy-done.6, f32[384,768]{1,0:T(8,128)} %copy-done.32), kind=kOutput, calls=%fused_computation.116 | convolution fusion | flops 453279744 | bytes 3538944 | tf_op jit(solution)/shard_map/dot_general | solution.py:22
  162.9 9.2 %attend_back.3 = (bf16[384,256]{1,0:T(8,128)(2,1)S(1)}, bf16[1536,256]{1,0:T(8,128)(2,1)S(1)}, bf16[1536,256]{1,0:T(8,128)(2,1)S(1)}) custom-call(bf16[384,768]{1,0:T(8,128)(2,1)S(1)} %get-tuple-element.38.q_ref, bf16[1536,768]{1,0:T(8,128)(2,1)} %copy-done, bf16[1536,768]{1,0:T(8,128)(2,1)} %copy-done.1, bf16[1536,128]{1,0:T(8,128)(2,1)S(1)} %select_convert_fusion.f_ref, ...), custom_call_target="tpu_custom_call" | custom-call | tf_op jit(solution)/shard_map/attend_back/pallas_call | solution.py:362
  173.2 3.7 %add_convert_fusion.after_ref = bf16[8,528,384]{2,1,0:T(8,128)(2,1)S(1)} fusion(bf16[8,528,384]{2,1,0:T(8,128)(2,1)} %collective-permute-done.18, bf16[8,528,384]{2,1,0:T(8,128)(2,1)} %get-tuple-element.107), kind=kLoop, calls=%fused_computation | loop fusion | flops 6488064 | bytes 9732096 | tf_op jit(solution)/shard_map/convert_element_type | solution.py:107
  181.4 9.0 %attend_back.4 = (bf16[384,256]{1,0:T(8,128)(2,1)S(1)}, bf16[1536,256]{1,0:T(8,128)(2,1)S(1)}, bf16[1536,256]{1,0:T(8,128)(2,1)S(1)}) custom-call(bf16[384,768]{1,0:T(8,128)(2,1)S(1)} %get-tuple-element.38.q_ref, bf16[1536,768]{1,0:T(8,128)(2,1)} %copy-done, bf16[1536,768]{1,0:T(8,128)(2,1)} %copy-done.1, bf16[1536,128]{1,0:T(8,128)(2,1)S(1)} %select_convert_fusion.f_ref, ...), custom_call_target="tpu_custom_call" | custom-call | tf_op jit(solution)/shard_map/attend_back/pallas_call | solution.py:362
  192.7 9.0 %attend_back.5 = (bf16[384,256]{1,0:T(8,128)(2,1)S(1)}, bf16[1536,256]{1,0:T(8,128)(2,1)S(1)}, bf16[1536,256]{1,0:T(8,128)(2,1)S(1)}) custom-call(bf16[384,768]{1,0:T(8,128)(2,1)S(1)} %get-tuple-element.38.q_ref, bf16[1536,768]{1,0:T(8,128)(2,1)} %copy-done, bf16[1536,768]{1,0:T(8,128)(2,1)} %copy-done.1, bf16[1536,128]{1,0:T(8,128)(2,1)S(1)} %select_convert_fusion.f_ref, ...), custom_call_target="tpu_custom_call" | custom-call | tf_op jit(solution)/shard_map/attend_back/pallas_call | solution.py:362
  205.7 5.9 %fusion = f32[1536,768]{1,0:T(8,128)S(1)} fusion(bf16[1536,1536]{1,0:T(8,128)(2,1)} %constant_dynamic-update-slice_fusion.25, bf16[768,2304]{1,0:T(8,128)(2,1)S(1)} %copy-done.57), kind=kOutput, calls=%fused_computation.10 | convolution fusion | flops 3623878656 | bytes 11796480 | tf_op jit(solution)/shard_map/dot_general | solution.py:22
  211.7 2.4 copy-done.40
  216.3 4.4 %convolution_convert_fusion.2 = bf16[768,1536]{1,0:T(8,128)(2,1)S(1)} fusion(bf16[1536,768]{1,0:T(8,128)(2,1)S(1)} %copy-done.27, bf16[1536,1536]{1,0:T(8,128)(2,1)S(1)} %copy-done.52), kind=kOutput, calls=%fused_computation.4 | convolution fusion | flops 3625058304 | bytes 9437184 | tf_op jit(solution)/shard_map/dot_general | solution.py:30
  221.5 6.8 %collective-permute-done.36 = bf16[528,384]{1,0:T(8,128)(2,1)S(1)} collective-permute-done((bf16[528,384]{1,0:T(8,128)(2,1)S(1)}, bf16[528,384]{1,0:T(8,128)(2,1)S(1)}, u32[]{:S(2)}, u32[]{:S(2)}) %collective-permute-start.36) | collective-permute-done | bytes 405536 | tf_op jit(solution)/shard_map/ppermute | solution.py:51
  229.5 11.0 %collective-permute-done.37 = bf16[528,384]{1,0:T(8,128)(2,1)S(1)} collective-permute-done((bf16[528,384]{1,0:T(8,128)(2,1)S(1)}, bf16[528,384]{1,0:T(8,128)(2,1)S(1)}, u32[]{:S(2)}, u32[]{:S(2)}) %collective-permute-start.37) | collective-permute-done | bytes 405536 | tf_op jit(solution)/shard_map/ppermute | solution.py:51
  240.7 1.6 collective-permute-start.38
  244.3 1.8 fusion.13
  246.1 7.0 %collective-permute-done.38 = bf16[528,384]{1,0:T(8,128)(2,1)S(1)} collective-permute-done((bf16[528,384]{1,0:T(8,128)(2,1)S(1)}, bf16[528,384]{1,0:T(8,128)(2,1)S(1)}, u32[]{:S(2)}, u32[]{:S(2)}) %collective-permute-start.38) | collective-permute-done | bytes 405536 | tf_op jit(solution)/shard_map/ppermute | solution.py:51
  253.3 9.2 %collective-permute-done.21 = bf16[1,384,768]{2,1,0:T(8,128)(2,1)S(1)} collective-permute-done((bf16[1,384,768]{2,1,0:T(8,128)(2,1)S(1)}, bf16[1,384,768]{2,1,0:T(8,128)(2,1)S(1)}, u32[]{:S(2)}, u32[]{:S(2)}) %collective-permute-start.21) | collective-permute-done | bytes 589856 | tf_op jit(solution)/shard_map/ppermute | solution.py:51
  269.7 2.9 collective-permute-done.26
  273.8 3.5 %collective-permute-done.25 = bf16[288,384]{1,0:T(8,128)(2,1)S(1)} collective-permute-done((bf16[288,384]{1,0:T(8,128)(2,1)S(1)}, bf16[288,384]{1,0:T(8,128)(2,1)S(1)}, u32[]{:S(2)}, u32[]{:S(2)}) %collective-permute-start.25) | collective-permute-done | bytes 221216 | tf_op jit(solution)/shard_map/ppermute | solution.py:51
  277.3 4.7 %collective-permute-done.27 = bf16[288,384]{1,0:T(8,128)(2,1)S(1)} collective-permute-done((bf16[288,384]{1,0:T(8,128)(2,1)S(1)}, bf16[288,384]{1,0:T(8,128)(2,1)S(1)}, u32[]{:S(2)}, u32[]{:S(2)}) %collective-permute-start.27) | collective-permute-done | bytes 221216 | tf_op jit(solution)/shard_map/ppermute | solution.py:51
  282.2 8.4 %collective-permute-done.28 = bf16[288,384]{1,0:T(8,128)(2,1)S(1)} collective-permute-done((bf16[288,384]{1,0:T(8,128)(2,1)S(1)}, bf16[288,384]{1,0:T(8,128)(2,1)S(1)}, u32[]{:S(2)}, u32[]{:S(2)}) %collective-permute-start.28) | collective-permute-done | bytes 221216 | tf_op jit(solution)/shard_map/ppermute | solution.py:51
  290.8 7.7 %collective-permute-done.29 = bf16[288,384]{1,0:T(8,128)(2,1)S(1)} collective-permute-done((bf16[288,384]{1,0:T(8,128)(2,1)S(1)}, bf16[288,384]{1,0:T(8,128)(2,1)S(1)}, u32[]{:S(2)}, u32[]{:S(2)}) %collective-permute-start.29) | collective-permute-done | bytes 221216 | tf_op jit(solution)/shard_map/ppermute | solution.py:51
  301.1 3.5 %collective-permute-done.30 = bf16[288,384]{1,0:T(8,128)(2,1)S(1)} collective-permute-done((bf16[288,384]{1,0:T(8,128)(2,1)S(1)}, bf16[288,384]{1,0:T(8,128)(2,1)S(1)}, u32[]{:S(2)}, u32[]{:S(2)}) %collective-permute-start.30) | collective-permute-done | bytes 221216 | tf_op jit(solution)/shard_map/ppermute | solution.py:51
  (304 shorter events, 76.3 us)
Async XLA Ops:
  0.6 15.3 %copy-start.44 = (bf16[96,2304]{1,0:T(8,128)(2,1)S(1)}, bf16[96,2304]{1,0:T(8,128)(2,1)}, u32[]{:S(2)}) copy-start(bf16[96,2304]{1,0:T(8,128)(2,1)} %param.17) | copy-start | bytes 1327108
  0.7 33.8 %copy-start.53 = (bf16[144,768]{1,0:T(8,128)(2,1)S(1)}, bf16[144,768]{1,0:T(8,128)(2,1)}, u32[]{:S(2)}) copy-start(bf16[144,768]{1,0:T(8,128)(2,1)} %param.18) | copy-start | bytes 663556
  3.2 38.3 %collective-permute-start.2 = (bf16[112,1152]{1,0:T(8,128)(2,1)}, bf16[112,1152]{1,0:T(8,128)(2,1)}, u32[]{:S(2)}, u32[]{:S(2)}) collective-permute-start(bf16[112,1152]{1,0:T(8,128)(2,1)} %pad_maximum_fusion.8), channel_id=1, source_target_pairs={{0,4},{1,5},{2,6},{3,7},{4,0},{5,1},{6,2},{7,3},{8,12},{9,13},{10,... | collective-permute-start | bytes 774152 | tf_op jit(solution)/shard_map/ppermute | solution.py:51
  6.1 9.8 %collective-permute-start.3 = (bf16[112,1152]{1,0:T(8,128)(2,1)}, bf16[112,1152]{1,0:T(8,128)(2,1)S(1)}, u32[]{:S(2)}, u32[]{:S(2)}) collective-permute-start(bf16[112,1152]{1,0:T(8,128)(2,1)} %pad_maximum_fusion.8), channel_id=1, source_target_pairs={{0,8},{1,9},{2,10},{3,11},{4,12},{5,13},{6,14},{7,15},{8,16},{9,17... | collective-permute-start | bytes 774152 | tf_op jit(solution)/shard_map/ppermute | solution.py:51
  11.1 77.5 %collective-permute-start = (bf16[1,400,768]{2,1,0:T(8,128)(2,1)}, bf16[1,400,768]{2,1,0:T(8,128)(2,1)}, u32[]{:S(2)}, u32[]{:S(2)}) collective-permute-start(bf16[1,400,768]{2,1,0:T(8,128)(2,1)} %maximum_bitcast_fusion), channel_id=1, source_target_pairs={{0,2},{1,3},{2,0},{3,1},{4,6},{5,7},{6,4},{7,5},{8,10},{9,11},{10,... | collective-permute-start | bytes 1843208 | tf_op jit(solution)/shard_map/ppermute | solution.py:51
  15.9 8.8 %collective-permute-start.5 = (bf16[112,1152]{1,0:T(8,128)(2,1)S(1)}, bf16[112,1152]{1,0:T(8,128)(2,1)}, u32[]{:S(2)}, u32[]{:S(2)}) collective-permute-start(bf16[112,1152]{1,0:T(8,128)(2,1)S(1)} %collective-permute-done.3), channel_id=1, source_target_pairs={{0,8},{1,9},{2,10},{3,11},{4,12},{5,13},{6,14},{7,15},{8,16},{9,17... | collective-permute-start | bytes 774152 | tf_op jit(solution)/shard_map/ppermute | solution.py:51
  24.7 8.3 %collective-permute-start.7 = (bf16[112,1152]{1,0:T(8,128)(2,1)}, bf16[112,1152]{1,0:T(8,128)(2,1)S(1)}, u32[]{:S(2)}, u32[]{:S(2)}) collective-permute-start(bf16[112,1152]{1,0:T(8,128)(2,1)} %collective-permute-done.5), channel_id=1, source_target_pairs={{0,8},{1,9},{2,10},{3,11},{4,12},{5,13},{6,14},{7,15},{8,16},{9,17... | collective-permute-start | bytes 774152 | tf_op jit(solution)/shard_map/ppermute | solution.py:51
  33.0 23.8 %copy-start.47 = (bf16[112,1152]{1,0:T(8,128)(2,1)}, bf16[112,1152]{1,0:T(8,128)(2,1)S(1)}, u32[]{:S(2)}) copy-start(bf16[112,1152]{1,0:T(8,128)(2,1)S(1)} %collective-permute-done.7) | copy-start | bytes 774148
  33.0 7.9 %collective-permute-start.8 = (bf16[112,1152]{1,0:T(8,128)(2,1)S(1)}, bf16[112,1152]{1,0:T(8,128)(2,1)S(1)}, u32[]{:S(2)}, u32[]{:S(2)}) collective-permute-start(bf16[112,1152]{1,0:T(8,128)(2,1)S(1)} %collective-permute-done.7), channel_id=1, source_target_pairs={{0,4},{1,5},{2,6},{3,7},{4,0},{5,1},{6,2},{7,3},{8,12},{9,13},{10,... | collective-permute-start | bytes 774152 | tf_op jit(solution)/shard_map/ppermute | solution.py:51
  40.9 15.9 %copy-start.49 = (bf16[112,1152]{1,0:T(8,128)(2,1)}, bf16[112,1152]{1,0:T(8,128)(2,1)S(1)}, u32[]{:S(2)}) copy-start(bf16[112,1152]{1,0:T(8,128)(2,1)S(1)} %collective-permute-done.8) | copy-start | bytes 774148
  40.9 12.6 %collective-permute-start.10 = (bf16[528,384]{1,0:T(8,128)(2,1)}, bf16[528,384]{1,0:T(8,128)(2,1)S(1)}, u32[]{:S(2)}, u32[]{:S(2)}) collective-permute-start(bf16[528,384]{1,0:T(8,128)(2,1)} %constant_dynamic-update-slice_fusion.9), channel_id=1, source_target_pairs={{0,8},{1,9},{2,10},{3,11},{4,12},{5,13},{6,14},{7,15},{8,16},{9,17... | collective-permute-start | bytes 1216520 | tf_op jit(solution)/shard_map/ppermute | solution.py:51
  41.0 15.7 %collective-permute-start.4 = (bf16[112,1152]{1,0:T(8,128)(2,1)}, bf16[112,1152]{1,0:T(8,128)(2,1)S(1)}, u32[]{:S(2)}, u32[]{:S(2)}) collective-permute-start(bf16[112,1152]{1,0:T(8,128)(2,1)} %copy-done.51), channel_id=1, source_target_pairs={{0,4},{1,5},{2,6},{3,7},{4,0},{5,1},{6,2},{7,3},{8,12},{9,13},{10,... | collective-permute-start | bytes 774152 | tf_op jit(solution)/shard_map/ppermute | solution.py:51
  53.6 13.7 %collective-permute-start.11 = (bf16[528,384]{1,0:T(8,128)(2,1)S(1)}, bf16[528,384]{1,0:T(8,128)(2,1)S(1)}, u32[]{:S(2)}, u32[]{:S(2)}) collective-permute-start(bf16[528,384]{1,0:T(8,128)(2,1)S(1)} %collective-permute-done.10.after_ref), channel_id=1, source_target_pairs={{0,8},{1,9},{2,10},{3,11},{4,12},{5,13},{6,14},{7,15},{8,16},{9,17... | collective-permute-start | bytes 1216520 | tf_op jit(solution)/shard_map/ppermute | solution.py:51
  54.6 37.0 %collective-permute-start.6 = (bf16[112,1152]{1,0:T(8,128)(2,1)}, bf16[112,1152]{1,0:T(8,128)(2,1)S(1)}, u32[]{:S(2)}, u32[]{:S(2)}) collective-permute-start(bf16[112,1152]{1,0:T(8,128)(2,1)} %collective-permute-done.5), channel_id=1, source_target_pairs={{0,4},{1,5},{2,6},{3,7},{4,0},{5,1},{6,2},{7,3},{8,12},{9,13},{10,... | collective-permute-start | bytes 774152 | tf_op jit(solution)/shard_map/ppermute | solution.py:51
  54.7 16.1 %collective-permute-start.13 = (bf16[528,384]{1,0:T(8,128)(2,1)}, bf16[528,384]{1,0:T(8,128)(2,1)S(1)}, u32[]{:S(2)}, u32[]{:S(2)}) collective-permute-start(bf16[528,384]{1,0:T(8,128)(2,1)} %constant_dynamic-update-slice_fusion.9), channel_id=1, source_target_pairs={{0,4},{1,5},{2,6},{3,7},{4,0},{5,1},{6,2},{7,3},{8,12},{9,13},{10,... | collective-permute-start | bytes 1216520 | tf_op jit(solution)/shard_map/ppermute | solution.py:51
  56.7 22.5 %collective-permute-start.14 = (bf16[528,384]{1,0:T(8,128)(2,1)S(1)}, bf16[528,384]{1,0:T(8,128)(2,1)S(1)}, u32[]{:S(2)}, u32[]{:S(2)}) collective-permute-start(bf16[528,384]{1,0:T(8,128)(2,1)S(1)} %collective-permute-done.10.after_ref), channel_id=1, source_target_pairs={{0,4},{1,5},{2,6},{3,7},{4,0},{5,1},{6,2},{7,3},{8,12},{9,13},{10,... | collective-permute-start | bytes 1216520 | tf_op jit(solution)/shard_map/ppermute | solution.py:51
  67.2 9.7 %collective-permute-start.12 = (bf16[528,384]{1,0:T(8,128)(2,1)S(1)}, bf16[528,384]{1,0:T(8,128)(2,1)S(1)}, u32[]{:S(2)}, u32[]{:S(2)}) collective-permute-start(bf16[528,384]{1,0:T(8,128)(2,1)S(1)} %collective-permute-done.11.after_ref), channel_id=1, source_target_pairs={{0,8},{1,9},{2,10},{3,11},{4,12},{5,13},{6,14},{7,15},{8,16},{9,17... | collective-permute-start | bytes 1216520 | tf_op jit(solution)/shard_map/ppermute | solution.py:51
  70.8 12.7 %collective-permute-start.15 = (bf16[528,384]{1,0:T(8,128)(2,1)S(1)}, bf16[528,384]{1,0:T(8,128)(2,1)S(1)}, u32[]{:S(2)}, u32[]{:S(2)}) collective-permute-start(bf16[528,384]{1,0:T(8,128)(2,1)S(1)} %collective-permute-done.11.after_ref), channel_id=1, source_target_pairs={{0,4},{1,5},{2,6},{3,7},{4,0},{5,1},{6,2},{7,3},{8,12},{9,13},{10,... | collective-permute-start | bytes 1216520 | tf_op jit(solution)/shard_map/ppermute | solution.py:51
  76.9 14.1 %copy-start.9 = (bf16[528,384]{1,0:T(8,128)(2,1)}, bf16[528,384]{1,0:T(8,128)(2,1)S(1)}, u32[]{:S(2)}) copy-start(bf16[528,384]{1,0:T(8,128)(2,1)S(1)} %collective-permute-done.12.after_ref) | copy-start | bytes 1216516
  76.9 10.9 %collective-permute-start.16 = (bf16[528,384]{1,0:T(8,128)(2,1)S(1)}, bf16[528,384]{1,0:T(8,128)(2,1)S(1)}, u32[]{:S(2)}, u32[]{:S(2)}) collective-permute-start(bf16[528,384]{1,0:T(8,128)(2,1)S(1)} %collective-permute-done.12.after_ref), channel_id=1, source_target_pairs={{0,4},{1,5},{2,6},{3,7},{4,0},{5,1},{6,2},{7,3},{8,12},{9,13},{10,... | collective-permute-start | bytes 1216520 | tf_op jit(solution)/shard_map/ppermute | solution.py:51
  88.7 46.1 %collective-permute-start.17 = (bf16[4224,384]{1,0:T(8,128)(2,1)}, bf16[4224,384]{1,0:T(8,128)(2,1)}, u32[]{:S(2)}, u32[]{:S(2)}) collective-permute-start(bf16[4224,384]{1,0:T(8,128)(2,1)} %constant_dynamic-update-slice_fusion.17.own_ref), channel_id=1, source_target_pairs={{0,1},{1,0},{2,3},{3,2},{4,5},{5,4},{6,7},{7,6},{8,9},{9,8},{10,11... | collective-permute-start | bytes 9732104 | tf_op jit(solution)/shard_map/ppermute | solution.py:51
  91.1 7.2 %collective-permute-start.1 = (bf16[2,400,768]{2,1,0:T(8,128)(2,1)}, bf16[2,400,768]{2,1,0:T(8,128)(2,1)}, u32[]{:S(2)}, u32[]{:S(2)}) collective-permute-start(bf16[2,400,768]{2,1,0:T(8,128)(2,1)} %pad_maximum_fusion.3), channel_id=1, source_target_pairs={{0,1},{1,0},{2,3},{3,2},{4,5},{5,4},{6,7},{7,6},{8,9},{9,8},{10,11... | collective-permute-start | bytes 3686408 | tf_op jit(solution)/shard_map/ppermute | solution.py:51
  91.7 13.1 %collective-permute-start.9 = (bf16[896,1152]{1,0:T(8,128)(2,1)S(1)}, bf16[896,1152]{1,0:T(8,128)(2,1)}, u32[]{:S(2)}, u32[]{:S(2)}) collective-permute-start(bf16[896,1152]{1,0:T(8,128)(2,1)S(1)} %constant_dynamic-update-slice_fusion.own_ref), channel_id=1, source_target_pairs={{0,1},{1,0},{2,3},{3,2},{4,5},{5,4},{6,7},{7,6},{8,9},{9,8},{10,11... | collective-permute-start | bytes 6193160 | tf_op jit(solution)/shard_map/ppermute | solution.py:51
  157.5 15.7 %collective-permute-start.18 = (bf16[8,528,384]{2,1,0:T(8,128)(2,1)}, bf16[8,528,384]{2,1,0:T(8,128)(2,1)}, u32[]{:S(2)}, u32[]{:S(2)}) collective-permute-start(bf16[8,528,384]{2,1,0:T(8,128)(2,1)} %get-tuple-element.108.after_ref), channel_id=1, source_target_pairs={{0,1},{1,0},{2,3},{3,2},{4,5},{5,4},{6,7},{7,6},{8,9},{9,8},{10,11... | collective-permute-start | bytes 9732104 | tf_op jit(solution)/shard_map/ppermute | solution.py:51
  177.2 14.3 %collective-permute-start.19 = (bf16[528,384]{1,0:T(8,128)(2,1)S(1)}, bf16[528,384]{1,0:T(8,128)(2,1)S(1)}, u32[]{:S(2)}, u32[]{:S(2)}) collective-permute-start(bf16[528,384]{1,0:T(8,128)(2,1)S(1)} %get-tuple-element.96), channel_id=1, source_target_pairs={{0,4},{1,5},{2,6},{3,7},{4,0},{5,1},{6,2},{7,3},{8,12},{9,13},{10,... | collective-permute-start | bytes 1216520 | tf_op jit(solution)/shard_map/ppermute | solution.py:51
  178.2 36.1 %collective-permute-start.34 = (bf16[528,384]{1,0:T(8,128)(2,1)S(1)}, bf16[528,384]{1,0:T(8,128)(2,1)S(1)}, u32[]{:S(2)}, u32[]{:S(2)}) collective-permute-start(bf16[528,384]{1,0:T(8,128)(2,1)S(1)} %get-tuple-element.94), channel_id=1, source_target_pairs={{0,4},{1,5},{2,6},{3,7},{4,0},{5,1},{6,2},{7,3},{8,12},{9,13},{10,... | collective-permute-start | bytes 1216520 | tf_op jit(solution)/shard_map/ppermute | solution.py:51
  179.4 42.1 %collective-permute-start.33 = (bf16[528,384]{1,0:T(8,128)(2,1)S(1)}, bf16[528,384]{1,0:T(8,128)(2,1)S(1)}, u32[]{:S(2)}, u32[]{:S(2)}) collective-permute-start(bf16[528,384]{1,0:T(8,128)(2,1)S(1)} %get-tuple-element.95), channel_id=1, source_target_pairs={{0,4},{1,5},{2,6},{3,7},{4,0},{5,1},{6,2},{7,3},{8,12},{9,13},{10,... | collective-permute-start | bytes 1216520 | tf_op jit(solution)/shard_map/ppermute | solution.py:51
  180.3 49.2 %collective-permute-start.32 = (bf16[528,384]{1,0:T(8,128)(2,1)S(1)}, bf16[528,384]{1,0:T(8,128)(2,1)S(1)}, u32[]{:S(2)}, u32[]{:S(2)}) collective-permute-start(bf16[528,384]{1,0:T(8,128)(2,1)S(1)} %get-tuple-element.93), channel_id=1, source_target_pairs={{0,4},{1,5},{2,6},{3,7},{4,0},{5,1},{6,2},{7,3},{8,12},{9,13},{10,... | collective-permute-start | bytes 1216520 | tf_op jit(solution)/shard_map/ppermute | solution.py:51
  192.6 21.7 %collective-permute-start.35 = (bf16[528,384]{1,0:T(8,128)(2,1)S(1)}, bf16[528,384]{1,0:T(8,128)(2,1)S(1)}, u32[]{:S(2)}, u32[]{:S(2)}) collective-permute-start(bf16[528,384]{1,0:T(8,128)(2,1)S(1)} %fusion.32.after_ref), channel_id=1, source_target_pairs={{0,8},{1,9},{2,10},{3,11},{4,12},{5,13},{6,14},{7,15},{8,16},{9,17... | collective-permute-start | bytes 1216520 | tf_op jit(solution)/shard_map/ppermute | solution.py:51
  214.2 28.0 %collective-permute-start.20 = (bf16[2,384,768]{2,1,0:T(8,128)(2,1)S(1)}, bf16[2,384,768]{2,1,0:T(8,128)(2,1)S(1)}, u32[]{:S(2)}, u32[]{:S(2)}) collective-permute-start(bf16[2,384,768]{2,1,0:T(8,128)(2,1)S(1)} %bitcast.120), channel_id=1, source_target_pairs={{0,1},{1,0},{2,3},{3,2},{4,5},{5,4},{6,7},{7,6},{8,9},{9,8},{10,11... | collective-permute-start | bytes 3538952 | tf_op jit(solution)/shard_map/ppermute | solution.py:51
  215.5 12.9 %collective-permute-start.36 = (bf16[528,384]{1,0:T(8,128)(2,1)S(1)}, bf16[528,384]{1,0:T(8,128)(2,1)S(1)}, u32[]{:S(2)}, u32[]{:S(2)}) collective-permute-start(bf16[528,384]{1,0:T(8,128)(2,1)S(1)} %fusion.28), channel_id=1, source_target_pairs={{0,8},{1,9},{2,10},{3,11},{4,12},{5,13},{6,14},{7,15},{8,16},{9,17... | collective-permute-start | bytes 1216520 | tf_op jit(solution)/shard_map/ppermute | solution.py:51
  228.5 12.0 %collective-permute-start.37 = (bf16[528,384]{1,0:T(8,128)(2,1)S(1)}, bf16[528,384]{1,0:T(8,128)(2,1)S(1)}, u32[]{:S(2)}, u32[]{:S(2)}) collective-permute-start(bf16[528,384]{1,0:T(8,128)(2,1)S(1)} %fusion.30), channel_id=1, source_target_pairs={{0,8},{1,9},{2,10},{3,11},{4,12},{5,13},{6,14},{7,15},{8,16},{9,17... | collective-permute-start | bytes 1216520 | tf_op jit(solution)/shard_map/ppermute | solution.py:51
  229.4 34.1 %collective-permute-start.22 = (bf16[8,288,384]{2,1,0:T(8,128)(2,1)S(1)}, bf16[8,288,384]{2,1,0:T(8,128)(2,1)S(1)}, u32[]{:S(2)}, u32[]{:S(2)}) collective-permute-start(bf16[8,288,384]{2,1,0:T(8,128)(2,1)S(1)} %pad_maximum_fusion.2), channel_id=1, source_target_pairs={{0,1},{1,0},{2,3},{3,2},{4,5},{5,4},{6,7},{7,6},{8,9},{9,8},{10,11... | collective-permute-start | bytes 5308424 | tf_op jit(solution)/shard_map/ppermute | solution.py:51
  240.7 12.4 %collective-permute-start.38 = (bf16[528,384]{1,0:T(8,128)(2,1)S(1)}, bf16[528,384]{1,0:T(8,128)(2,1)S(1)}, u32[]{:S(2)}, u32[]{:S(2)}) collective-permute-start(bf16[528,384]{1,0:T(8,128)(2,1)S(1)} %fusion.37), channel_id=1, source_target_pairs={{0,2},{1,3},{2,0},{3,1},{4,6},{5,7},{6,4},{7,5},{8,10},{9,11},{10,... | collective-permute-start | bytes 1216520 | tf_op jit(solution)/shard_map/ppermute | solution.py:51
  242.6 20.0 %collective-permute-start.21 = (bf16[1,384,768]{2,1,0:T(8,128)(2,1)S(1)}, bf16[1,384,768]{2,1,0:T(8,128)(2,1)S(1)}, u32[]{:S(2)}, u32[]{:S(2)}) collective-permute-start(bf16[1,384,768]{2,1,0:T(8,128)(2,1)S(1)} %slice.352), channel_id=1, source_target_pairs={{0,2},{1,3},{2,0},{3,1},{4,6},{5,7},{6,4},{7,5},{8,10},{9,11},{10,... | collective-permute-start | bytes 1769480 | tf_op jit(solution)/shard_map/ppermute | solution.py:51
  246.1 16.5 %copy-start.36 = (bf16[1,384,768]{2,1,0:T(8,128)(2,1)S(1)}, bf16[1,384,768]{2,1,0:T(8,128)(2,1)}, u32[]{:S(2)}) copy-start(bf16[1,384,768]{2,1,0:T(8,128)(2,1)} %param.10) | copy-start | bytes 1769476
  253.2 19.4 %collective-permute-start.39 = (bf16[528,384]{1,0:T(8,128)(2,1)S(1)}, bf16[528,384]{1,0:T(8,128)(2,1)S(1)}, u32[]{:S(2)}, u32[]{:S(2)}) collective-permute-start(bf16[528,384]{1,0:T(8,128)(2,1)S(1)} %get-tuple-element.74), channel_id=1, source_target_pairs={{0,1},{1,0},{2,3},{3,2},{4,5},{5,4},{6,7},{7,6},{8,9},{9,8},{10,11... | collective-permute-start | bytes 1216520 | tf_op jit(solution)/shard_map/ppermute | solution.py:51
  264.1 8.4 %collective-permute-start.26 = (bf16[288,384]{1,0:T(8,128)(2,1)S(1)}, bf16[288,384]{1,0:T(8,128)(2,1)S(1)}, u32[]{:S(2)}, u32[]{:S(2)}) collective-permute-start(bf16[288,384]{1,0:T(8,128)(2,1)S(1)} %get-tuple-element.100), channel_id=1, source_target_pairs={{0,4},{1,5},{2,6},{3,7},{4,0},{5,1},{6,2},{7,3},{8,12},{9,13},{10,... | collective-permute-start | bytes 663560 | tf_op jit(solution)/shard_map/ppermute | solution.py:51
  265.2 12.1 %collective-permute-start.25 = (bf16[288,384]{1,0:T(8,128)(2,1)S(1)}, bf16[288,384]{1,0:T(8,128)(2,1)S(1)}, u32[]{:S(2)}, u32[]{:S(2)}) collective-permute-start(bf16[288,384]{1,0:T(8,128)(2,1)S(1)} %get-tuple-element.101), channel_id=1, source_target_pairs={{0,4},{1,5},{2,6},{3,7},{4,0},{5,1},{6,2},{7,3},{8,12},{9,13},{10,... | collective-permute-start | bytes 663560 | tf_op jit(solution)/shard_map/ppermute | solution.py:51
  266.2 15.9 %collective-permute-start.24 = (bf16[288,384]{1,0:T(8,128)(2,1)S(1)}, bf16[288,384]{1,0:T(8,128)(2,1)S(1)}, u32[]{:S(2)}, u32[]{:S(2)}) collective-permute-start(bf16[288,384]{1,0:T(8,128)(2,1)S(1)} %get-tuple-element.102), channel_id=1, source_target_pairs={{0,4},{1,5},{2,6},{3,7},{4,0},{5,1},{6,2},{7,3},{8,12},{9,13},{10,... | collective-permute-start | bytes 663560 | tf_op jit(solution)/shard_map/ppermute | solution.py:51
  267.2 23.6 %collective-permute-start.23 = (bf16[288,384]{1,0:T(8,128)(2,1)S(1)}, bf16[288,384]{1,0:T(8,128)(2,1)S(1)}, u32[]{:S(2)}, u32[]{:S(2)}) collective-permute-start(bf16[288,384]{1,0:T(8,128)(2,1)S(1)} %get-tuple-element.99), channel_id=1, source_target_pairs={{0,4},{1,5},{2,6},{3,7},{4,0},{5,1},{6,2},{7,3},{8,12},{9,13},{10,... | collective-permute-start | bytes 663560 | tf_op jit(solution)/shard_map/ppermute | solution.py:51
  272.6 9.3 %collective-permute-start.27 = (bf16[288,384]{1,0:T(8,128)(2,1)S(1)}, bf16[288,384]{1,0:T(8,128)(2,1)S(1)}, u32[]{:S(2)}, u32[]{:S(2)}) collective-permute-start(bf16[288,384]{1,0:T(8,128)(2,1)S(1)} %fusion.38), channel_id=1, source_target_pairs={{0,8},{1,9},{2,10},{3,11},{4,12},{5,13},{6,14},{7,15},{8,16},{9,17... | collective-permute-start | bytes 663560 | tf_op jit(solution)/shard_map/ppermute | solution.py:51
  273.7 27.1 %copy-start.45 = (bf16[96,2304]{1,0:T(8,128)(2,1)S(1)}, bf16[96,2304]{1,0:T(8,128)(2,1)}, u32[]{:S(2)}) copy-start(bf16[96,2304]{1,0:T(8,128)(2,1)} %param.17) | copy-start | bytes 1327108
  282.1 8.5 %collective-permute-start.28 = (bf16[288,384]{1,0:T(8,128)(2,1)S(1)}, bf16[288,384]{1,0:T(8,128)(2,1)S(1)}, u32[]{:S(2)}, u32[]{:S(2)}) collective-permute-start(bf16[288,384]{1,0:T(8,128)(2,1)S(1)} %fusion.40), channel_id=1, source_target_pairs={{0,8},{1,9},{2,10},{3,11},{4,12},{5,13},{6,14},{7,15},{8,16},{9,17... | collective-permute-start | bytes 663560 | tf_op jit(solution)/shard_map/ppermute | solution.py:51
  290.7 7.8 %collective-permute-start.29 = (bf16[288,384]{1,0:T(8,128)(2,1)S(1)}, bf16[288,384]{1,0:T(8,128)(2,1)S(1)}, u32[]{:S(2)}, u32[]{:S(2)}) collective-permute-start(bf16[288,384]{1,0:T(8,128)(2,1)S(1)} %fusion.42), channel_id=1, source_target_pairs={{0,8},{1,9},{2,10},{3,11},{4,12},{5,13},{6,14},{7,15},{8,16},{9,17... | collective-permute-start | bytes 663560 | tf_op jit(solution)/shard_map/ppermute | solution.py:51
  290.8 14.0 %copy-start.58 = (bf16[96]{0:T(256)(128)(2,1)S(1)}, bf16[96]{0:T(256)(128)(2,1)}, u32[]{:S(2)}) copy-start(bf16[96]{0:T(256)(128)(2,1)} %param.16) | copy-start | bytes 580
  298.5 6.0 %collective-permute-start.30 = (bf16[288,384]{1,0:T(8,128)(2,1)S(1)}, bf16[288,384]{1,0:T(8,128)(2,1)S(1)}, u32[]{:S(2)}, u32[]{:S(2)}) collective-permute-start(bf16[288,384]{1,0:T(8,128)(2,1)S(1)} %fusion.47), channel_id=1, source_target_pairs={{0,2},{1,3},{2,0},{3,1},{4,6},{5,7},{6,4},{7,5},{8,10},{9,11},{10,... | collective-permute-start | bytes 663560 | tf_op jit(solution)/shard_map/ppermute | solution.py:51
  304.7 1.5 collective-permute-start.31
  (55 other events, 254.8 us)
